TPU v7x, 256 devices: a whole 4x4x8 slice. The times are simulated.
256 devices in a mesh: sec: 16 (over y, x), term: 16 (over z, core).
Axes of the slice: x: 4, y: 4, z: 8, core: 2. Of those that a mesh axis runs over, the one named last changes fastest.
Arguments:
- initial: float32 [8192, 512], P(('sec', 'term')), may hold values from -6 to 6
- onsite: float32 [8192, 512], P(('sec', 'term')), may hold values from 0.5 to 4
- left_env: float32 [16, 32, 512, 512], P('sec', 'term'), as said below
- right_env: float32 [16, 32, 512, 512], P('sec', 'term'), as said below
- sector_dims: int32 [16, 2], P('sec'), may hold values from 128 to 512, as said below
Outputs:
- block_vector: float32 [8192, 512], P(('sec', 'term'))
- energies: float32 [16], P('sec')
Inputs may be any that keep to these rules, and one draw needn't show every extreme that they name: `sector_dims`: at least one entry equals 512. `left_env`: each [section, term] matrix is symmetric. `right_env`: each [section, term] matrix is symmetric.
All inputs are finite; a program needn't handle non-finite values.
Results may differ from a plain program's by a relative error of at most 0.0003.
Values sent between devices are 32-bit elements; how exact they have to be, the bound alone decides.
A program may use at most 64 MiB of HBM per device.

v0:
```python
import jax
import jax.numpy as jnp
from jax import lax
from jax.sharding import PartitionSpec as P

ITERS = 4


def shifted(block, axis, distance):
    devices = range(lax.axis_size(axis))
    route = [(i - distance, i) for i in devices if i - distance in devices]
    return lax.ppermute(block, axis, route)


def advance(estimate, image, direction, turned, ritz_value, res_square, bend_value):
    half_gap = 0.5 * (bend_value - ritz_value)
    radius = jnp.sqrt(half_gap * half_gap + res_square)
    step_size = -jnp.sqrt(res_square) / (half_gap + radius)
    scale_back = jnp.sqrt(1.0 + step_size * step_size)
    new_estimate = (estimate + step_size * direction) / scale_back
    new_image = (image + step_size * turned) / scale_back
    return (new_estimate, new_image, ritz_value + half_gap - radius, step_size, scale_back)


def per_device(initial, onsite, left_env, right_env, sector_dims):
    row_count = initial.shape[0]
    width = initial.shape[1]
    left_terms = left_env[0]
    right_terms = shifted(right_env[0], "sec", -1)
    sector_pair = sector_dims[0]
    column_live = (jnp.arange(width) < sector_pair[1]).astype(jnp.float32)

    def carry_terms(vector_in):
        return jnp.einsum("ij,wjk->wik", vector_in, right_terms, precision=lax.Precision.HIGHEST)

    start_block, site_block = (
        lax.all_gather(initial, "term", axis=0, tiled=True),
        lax.all_gather(onsite, "term", axis=0, tiled=True),
    )
    row_live = (jnp.arange(width) < sector_pair[0]).astype(jnp.float32)
    live_mask = row_live[:, None] * column_live[None, :]

    def operate(vector_in):
        carried = carry_terms(vector_in)
        partial_sum = jnp.einsum(
            "wij,wjk->ik", left_terms, carried, precision=lax.Precision.HIGHEST
        )
        return live_mask * (lax.psum(partial_sum, "term") + site_block * vector_in)

    masked = live_mask * start_block
    estimate = masked / jnp.sqrt(jnp.sum(masked * masked))
    image = operate(estimate)
    ritz_value = jnp.sum(estimate * image)
    for iteration in range(ITERS):
        residual = image - ritz_value * estimate
        res_square = jnp.sum(residual * residual)
        direction = residual / jnp.sqrt(res_square)
        turned = operate(direction)
        bend_value = jnp.sum(direction * turned)
        estimate, image, ritz_value, step_size, scale_back = advance(
            estimate, image, direction, turned, ritz_value, res_square, bend_value
        )
    own_rows = lax.dynamic_slice_in_dim(estimate, lax.axis_index("term") * row_count, row_count, 0)
    return (own_rows * (0.5 * width), jnp.reshape(ritz_value, (1,)))


def solution(mesh):
    return jax.shard_map(
        per_device,
        mesh=mesh,
        in_specs=(
            P(("sec", "term"), None),
            P(("sec", "term"), None),
            P("sec", "term", None, None),
            P("sec", "term", None, None),
            P("sec", None),
        ),
        out_specs=(P(("sec", "term"), None), P("sec")),
        check_vma=False,
    )
```

profile of v0, /device:TPU:30, one launch (start us, length us, event | category | flops | bytes accessed | tf_op | source)
XLA Modules:
  0.0 744.5 jit_solution(4992532017257356242)
XLA Ops:
  8.0 4.1 collective-permute-start
  14.7 36.3 %all-gather.3.cloned.1.call-done = f32[512,512]{1,0:T(8,128)} async-done(((f32[32,512]{1,0:T(8,128)}), f32[512,512]{1,0:T(8,128)}) %all-gather.3.cloned.1.call-update) | async-done | bytes 1048592 | tf_op jit(solution)/shard_map/all_gather | solution.py:37
  55.9 5.4 fusion.50
  61.3 4.6 fusion.15
  66.4 23.7 %all-gather.5.cloned.1.call-done = f32[512,512]{1,0:T(8,128)} async-done(((f32[32,512]{1,0:T(8,128)}), f32[512,512]{1,0:T(8,128)}) %all-gather.5.cloned.1.call-update) | async-done | bytes 1048592 | tf_op jit(solution)/shard_map/all_gather | solution.py:38
  91.7 110.9 %all-reduce.6.cloned.1.call-done = f32[512,512]{0,1:T(8,128)} async-done(((f32[512,512]{0,1:T(8,128)}), f32[512,512]{0,1:T(8,128)}) %all-reduce.6.cloned.1.call-update) | async-done | bytes 1048592 | tf_op jit(solution)/shard_map/psum | solution.py:48
  208.8 6.8 fusion.48
  215.6 4.5 fusion.20
  220.4 111.5 %all-reduce.8.cloned.1.call-done = f32[512,512]{0,1:T(8,128)} async-done(((f32[512,512]{0,1:T(8,128)}), f32[512,512]{0,1:T(8,128)}) %all-reduce.8.cloned.1.call-update) | async-done | bytes 1048592 | tf_op jit(solution)/shard_map/psum | solution.py:48
  331.9 3.6 multiply_reduce_fusion.5
  338.1 5.1 multiply_reduce_fusion.4
  344.0 5.8 fusion.46
  349.7 4.6 fusion.25
  354.6 111.5 %all-reduce.10.cloned.1.call-done = f32[512,512]{0,1:T(8,128)} async-done(((f32[512,512]{0,1:T(8,128)}), f32[512,512]{0,1:T(8,128)}) %all-reduce.10.cloned.1.call-update) | async-done | bytes 1048592 | tf_op jit(solution)/shard_map/psum | solution.py:48
  466.1 3.0 multiply_reduce_fusion.3
  470.5 4.4 multiply_reduce_fusion.2
  475.5 5.8 fusion.44
  481.3 4.5 fusion.30
  486.2 111.4 %all-reduce.12.cloned.1.call-done = f32[512,512]{0,1:T(8,128)} async-done(((f32[512,512]{0,1:T(8,128)}), f32[512,512]{0,1:T(8,128)}) %all-reduce.12.cloned.1.call-update) | async-done | bytes 1048592 | tf_op jit(solution)/shard_map/psum | solution.py:48
  597.6 3.0 multiply_reduce_fusion.1
  602.0 4.3 multiply_reduce_fusion
  608.3 5.5 fusion.42
  613.8 4.6 fusion.35
  618.4 111.7 %all-reduce.14.cloned.1.call-done = f32[512,512]{0,1:T(8,128)} async-done(((f32[512,512]{0,1:T(8,128)}), f32[512,512]{0,1:T(8,128)}) %all-reduce.14.cloned.1.call-update) | async-done | bytes 1048592 | tf_op jit(solution)/shard_map/psum | solution.py:48
  (36 shorter events, 21.8 us)
Async XLA Ops:
  7.2 54.1 %copy-start = (f32[1,2,512,512]{3,2,1,0:T(8,128)S(1)}, f32[1,2,512,512]{3,2,1,0:T(8,128)}, u32[]{:S(2)}) copy-start(f32[1,2,512,512]{3,2,1,0:T(8,128)} %param.7) | copy-start | bytes 6291460
  7.2 43.9 %all-gather.3.cloned.1.call-start = ((), (), s32[]{:S(2)}) async-start(), calls=%async_computation | async-start | bytes 1114112 | tf_op jit(solution)/shard_map/all_gather | solution.py:37
  7.9 82.2 %all-gather.5.cloned.1.call-start = ((), (), s32[]{:S(2)}) async-start(), calls=%async_computation.2 | async-start | bytes 1114112 | tf_op jit(solution)/shard_map/all_gather | solution.py:38
  8.0 47.9 %collective-permute-start = (f32[2,512,512]{2,1,0:T(8,128)}, f32[2,512,512]{2,1,0:T(8,128)}, u32[]{:S(2)}, u32[]{:S(2)}) collective-permute-start(f32[2,512,512]{2,1,0:T(8,128)} %bitcast.90), channel_id=1, source_target_pairs={{16,0},{32,16},{48,32},{64,48},{80,64},{96,80},{112,96},{128,112},... | collective-permute-start | bytes 6291464 | tf_op jit(solution)/shard_map/ppermute | solution.py:12
  12.1 190.5 %all-reduce.6.cloned.1.call-start = ((), (), s32[]{:S(2)}) async-start(), calls=%async_computation.1 | async-start | bytes 2097152 | tf_op jit(solution)/shard_map/psum | solution.py:48
  52.6 8.7 %copy-start.1 = (f32[512,512]{0,1:T(8,128)}, f32[512,512]{0,1:T(8,128)S(1)}, u32[]{:S(2)}) copy-start(f32[512,512]{0,1:T(8,128)S(1)} %copy.10) | copy-start | bytes 3145732
  65.9 266.0 %all-reduce.8.cloned.1.call-start = ((), (), s32[]{:S(2)}) async-start(), calls=%async_computation.3 | async-start | bytes 2097152 | tf_op jit(solution)/shard_map/psum | solution.py:48
  202.6 3.8 copy-start.2
  205.3 1.0 copy-start.3
  220.1 245.9 %all-reduce.10.cloned.1.call-start = ((), (), s32[]{:S(2)}) async-start(), calls=%async_computation.4 | async-start | bytes 2097152 | tf_op jit(solution)/shard_map/psum | solution.py:48
  354.3 243.3 %all-reduce.12.cloned.1.call-start = ((), (), s32[]{:S(2)}) async-start(), calls=%async_computation.5 | async-start | bytes 2097152 | tf_op jit(solution)/shard_map/psum | solution.py:48
  485.9 244.3 %all-reduce.14.cloned.1.call-start = ((), (), s32[]{:S(2)}) async-start(), calls=%async_computation.6 | async-start | bytes 2097152 | tf_op jit(solution)/shard_map/psum | solution.py:48
  608.3 5.5 copy-start.4
Sparse Core Ops, SparseCore 0:
  9.8 41.1 all-gather.2
  52.9 37.1 all-gather.4
  92.5 110.0 all-reduce.5
  220.3 111.5 all-reduce.7
  354.5 111.5 all-reduce.9
  486.0 111.5 all-reduce.11
  618.5 111.5 all-reduce.13
where the time goes:
time: 752 us; the launch traced here: 745 us
  waiting for transfers between devices  619 us (82%)
  matrix products  52 us (7%)
  other arithmetic  35.2 us (5%)
  between operations  26.2 us (3%)
    psum x5, waiting for transfers between devices, operate(): return live_mask * (lax.psum(partial_sum, 'term') + site_block * vector_in)  557 us
    all_gather x1, waiting for transfers between devices, per_device(): lax.all_gather(initial, 'term', axis=0, tiled=True)  36.3 us
    dot_general x5, matrix products, carry_terms(): jnp.einsum('ij,wjk->wik', vector_in, right_terms, precision=lax.Precision...  29.2 us
    all_gather x1, waiting for transfers between devices, per_device(): lax.all_gather(onsite, 'term', axis=0, tiled=True)  23.7 us
    dot_general x5, matrix products, operate(): jnp.einsum('wij,wjk->ik', left_terms, carried, precision=lax.Precision.HI...  22.8 us
    reduce_sum x4, other arithmetic, per_device(): res_square = jnp.sum(residual * residual)  15.5 us
  transfers between devices with their start and end apart: 8, of which 8 were waited for; matrix products, arithmetic and copies ran while one was open for 2% of the time, Pallas kernels for 0%

commit v1 on v0

v1 whole, which is shorter than its diff:
```python
import functools

import jax
import jax.numpy as jnp
from jax import lax
from jax.experimental import pallas as pl
from jax.experimental.pallas import tpu as pltpu
from jax.sharding import PartitionSpec as P

ITERS = 4
PAD = 512
HALF = 256
TILE = 128
RING = 8
SECTIONS = 16
ROWS = PAD // RING
MESH = pl.DeviceIdType.MESH
F32, BF16 = jnp.float32, jnp.bfloat16


def dot(a, b):
    return jnp.dot(a, b, preferred_element_type=F32)


def split(x):
    high = x.astype(BF16)
    return high, (x - high.astype(F32)).astype(BF16)


def kernel(
    init_ref, site_ref, left_ref, right_ref, dims_ref, out_ref, energy_ref,
    lstage, lhi, llo, rdiag, roff, rhi, rlo, chi, clo,
    start, site, turned, estimate, image, resid, vhi, vlo, part, rsbuf, scal,
    lsem, lsend, lrecv, insend, inrecv, rsend, drecv, brecv, bfwd,
    rs_send, rs_recv, ag_send, ag_recv, cross_send, cross_recv, sc_send, sc_recv,
):
    s, t = lax.axis_index("sec"), lax.axis_index("term")
    z, c = t // 2, t % 2
    sign = 2 * c - 1

    def chip(k):
        return lax.rem(z + sign * k + 2 * RING, RING)

    def on_ring(k):
        return (s, chip(k) * 2 + c)

    other = (s, z * 2 + 1 - c)
    before = lax.rem(s + SECTIONS - 1, SECTIONS)
    after = lax.rem(s + 1, SECTIONS)

    def rows_of(chip_index):
        return pl.ds(pl.multiple_of(chip_index * ROWS, ROWS), ROWS)

    def remote(src, dst, send, recv, to):
        return pltpu.make_async_remote_copy(
            src_ref=src, dst_ref=dst, send_sem=send, recv_sem=recv,
            device_id=to, device_id_type=MESH,
        )

    local_left = [
        pltpu.make_async_copy(left_ref.at[0, j], lstage.at[2 * j], lsem.at[j])
        for j in range(2)
    ]
    for cp in local_left:
        cp.start()

    barrier = pltpu.get_barrier_semaphore()
    for k in range(1, 2 * RING):
        pl.semaphore_signal(
            barrier, inc=1, device_id=(s, lax.rem(t + k, 2 * RING)), device_id_type=MESH)
    for k in range(2):
        pl.semaphore_signal(
            barrier, inc=1, device_id=(after, z * 2 + k), device_id_type=MESH)
    pl.semaphore_wait(barrier, 2 * RING + 1)

    own_cols = pl.ds(pl.multiple_of(c * HALF, HALF), HALF)
    other_cols = pl.ds(pl.multiple_of((1 - c) * HALF, HALF), HALF)
    my_rows = pl.ds(pl.multiple_of(c * (ROWS // 2), ROWS // 2), ROWS // 2)
    peer_rows = pl.ds(pl.multiple_of((1 - c) * (ROWS // 2), ROWS // 2), ROWS // 2)
    inputs = [
        remote(ref.at[:, other_cols], buf.at[my_rows], insend.at[k], inrecv.at[k], other)
        for k, (ref, buf) in enumerate(((init_ref, start), (site_ref, site)))
    ]
    for cp in inputs:
        cp.start()

    def diag_copies(j, own):
        base = (c if own else 1 - c) * HALF
        slot = 2 * j + (0 if own else 1)
        to = (before, z * 2 + (c if own else 1 - c))
        out = []
        for m, (height, shift) in enumerate(((TILE, 0), (TILE, TILE))):
            r0 = pl.multiple_of(base + m * TILE, TILE)
            c0 = pl.multiple_of(base + shift, TILE)
            out.append(remote(
                right_ref.at[0, j, pl.ds(r0, height), pl.ds(c0, HALF - shift)],
                rdiag.at[slot, pl.ds(m * TILE, height), pl.ds(shift, HALF - shift)],
                rsend.at[j, 2 * (0 if own else 1) + m], drecv.at[slot, m], to))
        return out

    def off_copy(j):
        return remote(
            right_ref.at[0, j, pl.ds(0, HALF), pl.ds(HALF, HALF)], roff.at[2 * j],
            rsend.at[j, 4], brecv.at[2 * j], (before, t))

    def off_forward(j):
        return remote(
            roff.at[2 * j], roff.at[2 * j + 1], bfwd.at[j], brecv.at[2 * j + 1], other)

    shifts = [[off_copy(j)] + diag_copies(j, True) + diag_copies(j, False) for j in range(2)]
    for group in shifts:
        for cp in group:
            cp.start()
    left_cross = [
        remote(left_ref.at[0, j], lstage.at[2 * j + 1], lsend.at[j], lrecv.at[j], other)
        for j in range(2)
    ]
    for cp in left_cross:
        cp.start()

    row_index = lax.broadcasted_iota(jnp.int32, (ROWS, HALF), 0) + z * ROWS
    col_index = lax.broadcasted_iota(jnp.int32, (ROWS, HALF), 1) + c * HALF
    live = jnp.where(
        (row_index < dims_ref[0, 0]) & (col_index < dims_ref[0, 1]), 1.0, 0.0).astype(F32)

    own_rows = rows_of(z)

    def gather(n):
        def ring_copy(k, src_chip, index):
            part_ref = turned.at[n, 0, rows_of(src_chip)]
            return remote(part_ref, part_ref, ag_send.at[n, index], ag_recv.at[n, index],
                          on_ring(k))

        def cross_copy(k):
            return remote(turned.at[n, 0, rows_of(chip(k))], turned.at[n, 1, rows_of(chip(k))],
                          cross_send.at[n, k % RING], cross_recv.at[n, k % RING], other)

        def cross_wait(k):
            rows = rows_of(chip(-k))
            remote(turned.at[n, 0, rows], turned.at[n, 1, rows],
                   cross_send.at[n, k % RING], cross_recv.at[n, k % RING], other).wait_recv()

        plus2, minus2 = ring_copy(2, z, 0), ring_copy(-2, z, 1)
        plus1, minus1 = ring_copy(1, z, 2), ring_copy(-1, z, 3)
        for cp in (plus2, minus2, plus1, minus1):
            cp.start()
        sends = [plus2, minus2, plus1, minus1]

        def received(index, k):
            part_ref = turned.at[n, 0, rows_of(chip(k))]
            remote(part_ref, part_ref, ag_send.at[n, index], ag_recv.at[n, index],
                   on_ring(k)).wait_recv()

        crosses = [cross_copy(0)]
        crosses[-1].start()

        def cross(k):
            crosses.append(cross_copy(k))
            crosses[-1].start()

        received(0, -2)
        for cp in (ring_copy(1, chip(-2), 4), ring_copy(2, chip(-2), 5)):
            cp.start()
            sends.append(cp)
        received(1, 2)
        cp = ring_copy(-1, chip(2), 6)
        cp.start()
        sends.append(cp)
        cross(-2)
        cross(2)
        received(2, -1)
        cross(-1)
        received(3, 1)
        cross(1)
        received(4, -3)
        cross(-3)
        received(6, 3)
        cross(3)
        received(5, -4)
        cross(-4)
        for k in (0, -2, 2, -1, 1, -3, 3, -4):
            cross_wait(k)
        for cp in sends + crosses:
            cp.wait_send()

    def block(j):
        return part.at[pl.ds(j * ROWS, ROWS)]

    def reduce(n):
        def send(src, slot, k):
            cp = remote(src, rsbuf.at[n, slot], rs_send.at[n, slot], rs_recv.at[n, slot],
                        on_ring(k))
            cp.start()
            return cp

        def wait(slot):
            remote(block(0), rsbuf.at[n, slot], rs_send.at[n, slot], rs_recv.at[n, slot],
                   on_ring(1)).wait_recv()

        sends = [
            send(block(4), 1, 2), send(block(3), 0, 1), send(block(5), 2, -1),
            send(block(1), 3, 1), send(block(7), 4, -1),
        ]
        wait(0)
        wait(1)
        block(2)[...] = block(2)[...] + rsbuf[n, 0] + rsbuf[n, 1]
        sends.append(send(block(2), 5, 2))
        wait(2)
        block(6)[...] = block(6)[...] + rsbuf[n, 2]
        sends.append(send(block(6), 6, -2))
        wait(3)
        wait(4)
        total = block(0)[...] + rsbuf[n, 3] + rsbuf[n, 4]
        wait(5)
        wait(6)
        total = total + rsbuf[n, 5] + rsbuf[n, 6]
        for cp in sends:
            cp.wait_send()
        return total

    def carry(q):
        acc = (dot(vhi[0], rhi[q, 0]) + dot(vhi[1], rhi[q, 1])
               + dot(vlo[0], rhi[q, 0]) + dot(vlo[1], rhi[q, 1])
               + dot(vhi[0], rlo[q, 0]) + dot(vhi[1], rlo[q, 1]))
        chi[q], clo[q] = split(acc)

    def bring_back(q):
        return dot(lhi[q], chi[q]) + dot(llo[q], chi[q]) + dot(lhi[q], clo[q])

    def operate():
        for q in range(4):
            carry(q)
        part[...] = (bring_back(0) + bring_back(1)) + (bring_back(2) + bring_back(3))

    CHUNK = 64

    def over_chunks(body, sums):
        totals = [[], []]
        for half in range(2):
            def step(i, acc, half=half):
                rows = pl.ds(pl.multiple_of(i * CHUNK, CHUNK), CHUNK)
                values = body(half, rows)
                return tuple(
                    a + jnp.sum(v.reshape(CHUNK // 8, 8, HALF), axis=0)
                    for a, v in zip(acc, values))
            zero = tuple(jnp.zeros((8, HALF), F32) for _ in range(sums))
            acc = lax.fori_loop(0, PAD // CHUNK, step, zero, unroll=2)
            totals[half] = [jnp.sum(a, axis=(0, 1), keepdims=True) for a in acc]
        return [a + b for a, b in zip(*totals)]

    for cp in inputs:
        cp.wait_send()
    inputs_in = [
        remote(buf.at[peer_rows], buf.at[peer_rows], insend.at[k], inrecv.at[k], other)
        for k, buf in enumerate((start, site))
    ]
    for cp in inputs_in:
        cp.wait_recv()
    start[my_rows] = init_ref[:, own_cols]
    turned[0, 0, own_rows] = live * start[...]
    site[my_rows] = site_ref[:, own_cols]
    gather(0)

    def first_split(half, rows):
        u = turned[0, half, rows]
        vhi[half, rows], vlo[half, rows] = split(u)
        return (u * u,)

    (norm_square,) = over_chunks(first_split, 1)

    for j in range(2):
        local_left[j].wait()
        left_cross[j].wait()
    for q in range(4):
        for k in range(RING):
            hi, lo = split(lstage[q, rows_of(chip(k))])
            lhi[q, pl.ds(k * ROWS, ROWS)] = hi
            llo[q, pl.ds(k * ROWS, ROWS)] = lo

    present = jnp.where(s + 1 < SECTIONS, 1.0, 0.0).astype(F32)

    def prepare(q):
        for m, shift in ((0, 0), (1, TILE)):
            piece = rdiag.at[q, pl.ds(m * TILE, TILE), pl.ds(shift, HALF - shift)]
            remote(piece, piece, rsend.at[0, 0], drecv.at[q, m], other).wait_recv()
        top = rdiag[q, pl.ds(0, TILE), :] * present
        low = rdiag[q, pl.ds(TILE, TILE), pl.ds(TILE, TILE)] * present
        hi, lo = split(top)
        rhi[q, 0, pl.ds(0, TILE), :] = hi
        rlo[q, 0, pl.ds(0, TILE), :] = lo
        hi, lo = split(top[:, TILE:].T)
        rhi[q, 0, pl.ds(TILE, TILE), pl.ds(0, TILE)] = hi
        rlo[q, 0, pl.ds(TILE, TILE), pl.ds(0, TILE)] = lo
        hi, lo = split(low)
        rhi[q, 0, pl.ds(TILE, TILE), pl.ds(TILE, TILE)] = hi
        rlo[q, 0, pl.ds(TILE, TILE), pl.ds(TILE, TILE)] = lo

        @pl.when(c == 0)
        def _():
            rhi[q, 1], rlo[q, 1] = split((roff[q] * present).T)

        @pl.when(c == 1)
        def _():
            rhi[q, 1], rlo[q, 1] = split(roff[q] * present)

    for j in range(2):
        off_copy(j).wait_recv()
        forward = off_forward(j)
        forward.start()
        prepare(2 * j)
        carry(2 * j)
        forward.wait()
        prepare(2 * j + 1)
        carry(2 * j + 1)
        fresh = bring_back(2 * j) + bring_back(2 * j + 1)
        if j == 0:
            part[...] = fresh
        else:
            part[...] = part[...] + fresh
    for group in shifts:
        for cp in group:
            cp.wait_send()

    def image_rows(n, vector):
        own = reduce(n)
        turned[n + 1, 0, own_rows] = live * (own + site[...] * vector)
        gather(n + 1)

    image_rows(0, turned[0, 0, own_rows])
    inverse = 1.0 / jnp.sqrt(norm_square)

    def first_ritz(half, rows):
        est = turned[0, half, rows] * inverse
        img = turned[1, half, rows] * inverse
        estimate[half, rows] = est
        image[half, rows] = img
        return (est * img,)

    (ritz,) = over_chunks(first_ritz, 1)

    def first_residual(half, rows):
        res = image[half, rows] - ritz * estimate[half, rows]
        resid[half, rows] = res
        vhi[half, rows], vlo[half, rows] = split(res)
        return (res * res,)

    (res_square,) = over_chunks(first_residual, 1)

    def coefficients(ritz, res_square, bend):
        half_gap = 0.5 * (bend - ritz)
        radius = jnp.sqrt(half_gap * half_gap + res_square)
        step = -jnp.sqrt(res_square) / (half_gap + radius)
        back = 1.0 / jnp.sqrt(1.0 + step * step)
        return step, back, ritz + half_gap - radius

    def iterate(n, carried):
        ritz, res_square = carried
        operate()
        image_rows(n, resid[0, own_rows])
        inverse = 1.0 / jnp.sqrt(res_square)

        def bends(half, rows):
            return ((resid[half, rows] * inverse) * (turned[n + 1, half, rows] * inverse),)

        (bend,) = over_chunks(bends, 1)
        step, back, new_ritz = coefficients(ritz, res_square, bend)
        scaled = step * inverse

        def update(half, rows):
            est = (estimate[half, rows] + scaled * resid[half, rows]) * back
            img = (image[half, rows] + scaled * turned[n + 1, half, rows]) * back
            estimate[half, rows] = est
            image[half, rows] = img
            res = img - new_ritz * est
            resid[half, rows] = res
            vhi[half, rows], vlo[half, rows] = split(res)
            return (res * res,)

        (new_square,) = over_chunks(update, 1)
        return new_ritz, new_square

    ritz, res_square = lax.fori_loop(1, ITERS, iterate, (ritz, res_square))

    operate()
    inverse = 1.0 / jnp.sqrt(res_square)
    acc = site[...] * (resid[0, own_rows] * inverse) * (resid[0, own_rows] * inverse)
    for k in range(RING):
        acc = acc + (block(k)[...] * inverse) * (resid[0, rows_of(chip(k))] * inverse)
    mine = jnp.sum(acc, axis=(0, 1), keepdims=True)
    scal[t] = jnp.broadcast_to(mine, (8, 128))
    bends = []
    for k in range(1, 2 * RING):
        cp = remote(scal.at[t], scal.at[t], sc_send.at[k], sc_recv.at[k],
                    (s, lax.rem(t + k, 2 * RING)))
        cp.start()
        bends.append(cp)
    for k in range(1, 2 * RING):
        slot = scal.at[lax.rem(t + 2 * RING - k, 2 * RING)]
        remote(slot, slot, sc_send.at[k], sc_recv.at[k], other).wait_recv()
    bend = jnp.sum(scal[...], axis=0)[0:1, 0:1]
    step, back, ritz = coefficients(ritz, res_square, bend)
    scaled = step * inverse
    out_rows = pl.ds(pl.multiple_of(t * (ROWS // 2), ROWS // 2), ROWS // 2)
    for half, cols in ((0, own_cols), (1, other_cols)):
        est = (estimate[half, out_rows] + scaled * resid[half, out_rows]) * back
        out_ref[:, cols] = est * (0.5 * PAD)
    energy_ref[0] = ritz[0, 0]
    for cp in bends:
        cp.wait_send()


def per_device(initial, onsite, left_env, right_env, sector_dims):
    vmem = pl.BlockSpec(memory_space=pltpu.VMEM)
    smem = pl.BlockSpec(memory_space=pltpu.SMEM)
    anywhere = pl.BlockSpec(memory_space=pl.ANY)
    dma = pltpu.SemaphoreType.DMA
    full = (2, PAD, HALF)
    return pl.pallas_call(
        kernel,
        out_shape=(
            jax.ShapeDtypeStruct((ROWS // 2, PAD), F32),
            jax.ShapeDtypeStruct((1,), F32),
        ),
        in_specs=[vmem, vmem, anywhere, anywhere, smem],
        out_specs=(vmem, smem),
        scratch_shapes=[
            pltpu.VMEM((4, PAD, PAD), F32),
            pltpu.VMEM((4, PAD, PAD), BF16),
            pltpu.VMEM((4, PAD, PAD), BF16),
            pltpu.VMEM((4, HALF, HALF), F32),
            pltpu.VMEM((4, HALF, HALF), F32),
            pltpu.VMEM((4, 2, HALF, HALF), BF16),
            pltpu.VMEM((4, 2, HALF, HALF), BF16),
            pltpu.VMEM((4, PAD, HALF), BF16),
            pltpu.VMEM((4, PAD, HALF), BF16),
            pltpu.VMEM((ROWS, HALF), F32),
            pltpu.VMEM((ROWS, HALF), F32),
            pltpu.VMEM((ITERS + 1,) + full, F32),
            pltpu.VMEM(full, F32),
            pltpu.VMEM(full, F32),
            pltpu.VMEM(full, F32),
            pltpu.VMEM(full, BF16),
            pltpu.VMEM(full, BF16),
            pltpu.VMEM((PAD, HALF), F32),
            pltpu.VMEM((ITERS, 7, ROWS, HALF), F32),
            pltpu.VMEM((2 * RING, 8, 128), F32),
            dma((2,)), dma((2,)), dma((2,)), dma((2,)), dma((2,)),
            dma((2, 5)), dma((4, 2)), dma((4,)), dma((2,)),
            dma((ITERS, 7)), dma((ITERS, 7)),
            dma((ITERS + 1, 7)), dma((ITERS + 1, 7)),
            dma((ITERS + 1, RING)), dma((ITERS + 1, RING)),
            dma((2 * RING,)), dma((2 * RING,)),
        ],
        compiler_params=pltpu.CompilerParams(
            collective_id=0, has_side_effects=True, vmem_limit_bytes=56 * 2**20),
        cost_estimate=pl.CostEstimate(
            flops=5 * 3 * 2 * 4 * 2 * PAD * PAD * HALF, bytes_accessed=2**23, transcendentals=0),
    )(initial, onsite, left_env, right_env, sector_dims)


def solution(mesh):
    return jax.shard_map(
        per_device,
        mesh=mesh,
        in_specs=(
            P(("sec", "term"), None),
            P(("sec", "term"), None),
            P("sec", "term", None, None),
            P("sec", "term", None, None),
            P("sec", None),
        ),
        out_specs=(P(("sec", "term"), None), P("sec")),
        check_vma=False,
    )
```

time: 752 us -> 166 us (0.22)
  waiting for transfers between devices: 619 us -> 0 us
  Pallas kernels: 0 us -> 160 us
  matrix products: 52 us -> 0 us
  other arithmetic: 35.2 us -> 0 us
  between operations: 26.2 us -> 2.39 us
    psum x5 -> x0, waiting for transfers between devices: 557 us -> none  [operate(): return live_mask * (lax.psum(partial_sum, 'term') + site_block * vector_in)]
    pallas_call x0 -> x1, Pallas kernels: none -> 160 us  [per_device(): pl.pallas_call(kernel, out_shape=(jax.ShapeDtypeStruct((ROWS // 2, PAD),...]
    all_gather x2 -> x0, waiting for transfers between devices: 60.1 us -> none  [the longest x1 36.3 us: per_device(): lax.all_gather(initial, 'term', axis=0, tiled=True)]
    dot_general x10 -> x0, matrix products: 52 us -> none  [the longest x5 29.2 us: carry_terms(): jnp.einsum('ij,wjk->wik', vector_in, right_terms, precision=lax.Precision...]
    reduce_sum x10 -> x0, other arithmetic: 31.4 us -> none  [the longest x4 15.5 us: per_device(): res_square = jnp.sum(residual * residual)]
  transfers between devices with their start and end apart: 8 -> 0, of which waited for: 8 -> 0; matrix products, arithmetic and copies ran while one was open for 2% -> 0% of each run, Pallas kernels for 0% -> 0%
where the time goes in v1:
time: 166 us; the launch traced here: 164 us
  Pallas kernels  160 us (96%)
  between operations  2.39 us (1%)
    pallas_call x1, Pallas kernels, per_device(): pl.pallas_call(kernel, out_shape=(jax.ShapeDtypeStruct((ROWS // 2, PAD),...  160 us

profile of v1, /device:TPU:30, one launch (start us, length us, event | category | flops | bytes accessed | tf_op | source)
XLA Modules:
  0.0 164.1 jit_solution(5526122405398340402)
XLA Ops:
  0.6 160.2 %shard_map.68 = (f32[32,512]{1,0:T(8,128)}, f32[1]{0:T(128)}) custom-call(f32[32,512]{1,0:T(8,128)} %init_ref.1, f32[32,512]{1,0:T(8,128)} %site_ref.1, f32[1,2,512,512]{3,2,1,0:T(8,128)} %left_ref.1, f32[1,2,512,512]{3,2,1,0:T(8,128)} %right_ref.1, s32[1,2]{1,0:T(1,128)} %dims_ref.1), custom_call_target="tpu_custom_call" | custom-call | flops 16106127360 | bytes 8388608 | tf_op jit(solution)/shard_map/pallas_call | solution.py:418
  160.9 1.5 copy.9

commit v2 on v1

v2 whole, which is shorter than its diff:
```python
import functools

import jax
import jax.numpy as jnp
from jax import lax
from jax.experimental import pallas as pl
from jax.experimental.pallas import tpu as pltpu
from jax.sharding import PartitionSpec as P

ITERS = 4
PAD = 512
HALF = 256
TILE = 128
RING = 8
SECTIONS = 16
ROWS = PAD // RING
MESH = pl.DeviceIdType.MESH
F32, BF16 = jnp.float32, jnp.bfloat16


def dot(a, b):
    return jnp.dot(a, b, preferred_element_type=F32)


def split(x):
    high = x.astype(BF16)
    return high, (x - high.astype(F32)).astype(BF16)


def kernel(
    init_ref, site_ref, left_ref, right_ref, dims_ref, out_ref, energy_ref,
    lstage, lhi, llo, rdiag, roff, rhi, rlo, chi, clo,
    start, site, turned, estimate, image, resid, vhi, vlo, part, rsbuf, scal,
    lsem, lsend, lrecv, insend, inrecv, rsend, drecv, brecv, bfwd,
    rs_send, rs_recv, ag_send, ag_recv, cross_send, cross_recv, sc_send, sc_recv,
):
    s, t = lax.axis_index("sec"), lax.axis_index("term")
    z, c = t // 2, t % 2
    sign = 2 * c - 1

    def chip(k):
        return lax.rem(z + sign * k + 2 * RING, RING)

    def on_ring(k):
        return (s, chip(k) * 2 + c)

    other = (s, z * 2 + 1 - c)
    before = lax.rem(s + SECTIONS - 1, SECTIONS)
    after = lax.rem(s + 1, SECTIONS)

    def rows_of(chip_index):
        return pl.ds(pl.multiple_of(chip_index * ROWS, ROWS), ROWS)

    def remote(src, dst, send, recv, to):
        return pltpu.make_async_remote_copy(
            src_ref=src, dst_ref=dst, send_sem=send, recv_sem=recv,
            device_id=to, device_id_type=MESH,
        )

    local_left = [
        pltpu.make_async_copy(left_ref.at[0, j], lstage.at[2 * j], lsem.at[j])
        for j in range(2)
    ]
    for cp in local_left:
        cp.start()

    barrier = pltpu.get_barrier_semaphore()
    for k in range(1, 2 * RING):
        pl.semaphore_signal(
            barrier, inc=1, device_id=(s, lax.rem(t + k, 2 * RING)), device_id_type=MESH)
    for k in range(2):
        pl.semaphore_signal(
            barrier, inc=1, device_id=(after, z * 2 + k), device_id_type=MESH)
    pl.semaphore_wait(barrier, 2 * RING + 1)

    own_cols = pl.ds(pl.multiple_of(c * HALF, HALF), HALF)
    other_cols = pl.ds(pl.multiple_of((1 - c) * HALF, HALF), HALF)
    my_rows = pl.ds(pl.multiple_of(c * (ROWS // 2), ROWS // 2), ROWS // 2)
    peer_rows = pl.ds(pl.multiple_of((1 - c) * (ROWS // 2), ROWS // 2), ROWS // 2)
    inputs = [
        remote(ref.at[:, other_cols], buf.at[my_rows], insend.at[k], inrecv.at[k], other)
        for k, (ref, buf) in enumerate(((init_ref, start), (site_ref, site)))
    ]
    for cp in inputs:
        cp.start()

    def diag_copy(j, own, piece):
        column = c if own else 1 - c
        slot = 2 * j + (0 if own else 1)
        r0 = pl.multiple_of(column * HALF + piece * TILE, TILE)
        width = HALF - piece * TILE
        return remote(
            right_ref.at[0, j, pl.ds(r0, TILE), pl.ds(r0, width)],
            rdiag.at[slot, pl.ds(piece * TILE, TILE), pl.ds(piece * TILE, width)],
            rsend.at[j, (0 if own else 2) + piece], drecv.at[slot, piece],
            (before, z * 2 + column))

    off_parts = ((0, 0, HALF), (TILE, 0, TILE), (TILE, TILE, TILE))

    def off_piece(slot, piece):
        r0, c0, width = off_parts[piece]
        return roff.at[slot, pl.ds(r0, TILE), pl.ds(c0, width)]

    def off_copy(j, piece):
        r0, c0, width = off_parts[piece]
        return remote(
            right_ref.at[0, j, pl.ds(r0, TILE), pl.ds(HALF + c0, width)],
            off_piece(2 * j, piece), rsend.at[j, 4 + piece], brecv.at[2 * j, piece],
            (before, t))

    def off_forward(j, piece):
        return remote(off_piece(2 * j, piece), off_piece(2 * j + 1, piece),
                      bfwd.at[j, piece], brecv.at[2 * j + 1, piece], other)

    shifts = []
    for j in range(2):
        shifts += [off_copy(j, 0), off_copy(j, 1), diag_copy(j, True, 0), diag_copy(j, False, 0)]
    for j in range(2):
        shifts += [off_copy(j, 2), diag_copy(j, True, 1), diag_copy(j, False, 1)]
    for cp in shifts:
        cp.start()
    left_cross = [
        remote(left_ref.at[0, j], lstage.at[2 * j + 1], lsend.at[j], lrecv.at[j], other)
        for j in range(2)
    ]
    for cp in left_cross:
        cp.start()

    row_index = lax.broadcasted_iota(jnp.int32, (ROWS, HALF), 0) + z * ROWS
    col_index = lax.broadcasted_iota(jnp.int32, (ROWS, HALF), 1) + c * HALF
    live = jnp.where(
        (row_index < dims_ref[0, 0]) & (col_index < dims_ref[0, 1]), 1.0, 0.0).astype(F32)

    own_rows = rows_of(z)

    def gather_start(n, u):
        def ring_copy(k, src_chip, index):
            piece = turned.at[n, 0, u, rows_of(src_chip)]
            return remote(piece, piece, ag_send.at[n, u], ag_recv.at[n, u, index], on_ring(k))

        def cross(k):
            rows = rows_of(chip(k))
            remote(turned.at[n, 0, u, rows], turned.at[n, 1, u, rows],
                   cross_send.at[n, u], cross_recv.at[n, u], other).start()

        def received(index, k):
            piece = turned.at[n, 0, u, rows_of(chip(k))]
            remote(piece, piece, ag_send.at[n, u], ag_recv.at[n, u, index],
                   on_ring(k)).wait_recv()

        ring_copy(2, z, 0).start()
        ring_copy(-2, z, 1).start()
        ring_copy(1, z, 2).start()
        ring_copy(-1, z, 3).start()
        cross(0)

        def forward():
            received(0, -2)
            ring_copy(2, chip(-2), 5).start()
            ring_copy(1, chip(-2), 4).start()
            received(1, 2)
            ring_copy(-1, chip(2), 6).start()
            cross(-2)
            cross(2)
            received(2, -1)
            cross(-1)
            received(3, 1)
            cross(1)

        def finish():
            received(4, -3)
            cross(-3)
            received(6, 3)
            cross(3)
            received(5, -4)
            cross(-4)
            other_half = turned.at[n, 1, u]
            remote(other_half, other_half, cross_send.at[n, u], cross_recv.at[n, u],
                   other).wait_recv()

        return forward, finish

    def gather_sent(n, u):
        seven = rsbuf.at[0, 0]
        remote(seven, seven, ag_send.at[n, u], ag_recv.at[n, u, 0], other).wait_send()
        half = turned.at[n, 0, u]
        remote(half, half, cross_send.at[n, u], cross_recv.at[n, u], other).wait_send()

    def block(u, j):
        return part.at[u, pl.ds((j + 6) % RING * ROWS, ROWS)]

    def reduce_send(n, u, src, slot, k):
        remote(src, rsbuf.at[n, u, slot], rs_send.at[n, u], rs_recv.at[n, u, slot],
               on_ring(k)).start()

    def reduce_wait(n, u, slot):
        piece = rsbuf.at[n, u, slot]
        remote(piece, piece, rs_send.at[n, u], rs_recv.at[n, u, slot], on_ring(1)).wait_recv()

    def reduce_far(n, u):
        reduce_send(n, u, block(u, 4), 1, 2)
        reduce_send(n, u, block(u, 3), 0, 1)
        reduce_send(n, u, block(u, 5), 2, -1)

    def reduce_near(n, u):
        reduce_send(n, u, block(u, 1), 3, 1)
        reduce_send(n, u, block(u, 7), 4, -1)

    def reduce_relay(n, u):
        reduce_wait(n, u, 0)
        reduce_wait(n, u, 1)
        block(u, 2)[...] = block(u, 2)[...] + rsbuf[n, u, 0] + rsbuf[n, u, 1]
        reduce_send(n, u, block(u, 2), 5, 2)
        reduce_wait(n, u, 2)
        block(u, 6)[...] = block(u, 6)[...] + rsbuf[n, u, 2]
        reduce_send(n, u, block(u, 6), 6, -2)

    def reduce_final(n, u):
        reduce_wait(n, u, 3)
        reduce_wait(n, u, 4)
        total = block(u, 0)[...] + rsbuf[n, u, 3] + rsbuf[n, u, 4]
        reduce_wait(n, u, 5)
        reduce_wait(n, u, 6)
        return total + rsbuf[n, u, 5] + rsbuf[n, u, 6]

    def reduce_sent(n, u):
        seven = rsbuf.at[n, u]
        remote(seven, seven, rs_send.at[n, u], rs_recv.at[n, u, 0], other).wait_send()

    def own_image(n, u, vector):
        cols = slice(u * TILE, (u + 1) * TILE)
        turned[n + 1, 0, u, own_rows] = live[:, cols] * (
            reduce_final(n, u) + site[:, cols] * vector)

    def carry(q, cols):
        a, b = rhi[q, 0, :, cols], rhi[q, 1, :, cols]
        acc = (dot(vhi[0], a) + dot(vhi[1], b) + dot(vlo[0], a) + dot(vlo[1], b)
               + dot(vhi[0], rlo[q, 0, :, cols]) + dot(vhi[1], rlo[q, 1, :, cols]))
        chi[q, :, cols], clo[q, :, cols] = split(acc)

    def bring_back(rows, cols):
        terms = [
            dot(lhi[q, rows], chi[q, :, cols]) + dot(llo[q, rows], chi[q, :, cols])
            + dot(lhi[q, rows], clo[q, :, cols])
            for q in range(4)
        ]
        return (terms[0] + terms[1]) + (terms[2] + terms[3])

    far_rows, near_rows = slice(0, HALF), slice(HALF, PAD)
    every = slice(0, HALF)

    def operate(after_far):
        for q in range(4):
            carry(q, every)
        for rows, then in ((far_rows, after_far), (near_rows, None)):
            fresh = bring_back(rows, every)
            for u in range(2):
                part[u, rows] = fresh[:, u * TILE:(u + 1) * TILE]
            if then is not None:
                then()

    CHUNK = 128

    def over_chunks(body, sums):
        totals = [[], []]
        for half in range(2):
            def step(i, acc, half=half):
                rows = pl.ds(pl.multiple_of(i * CHUNK, CHUNK), CHUNK)
                for u in range(2):
                    values = body(half, u, rows)
                    acc = tuple(
                        a + jnp.sum(v.reshape(CHUNK // 8, 8, TILE), axis=0)
                        for a, v in zip(acc, values))
                return acc
            zero = tuple(jnp.zeros((8, TILE), F32) for _ in range(sums))
            acc = lax.fori_loop(0, PAD // CHUNK, step, zero)
            totals[half] = [jnp.sum(a, axis=(0, 1), keepdims=True) for a in acc]
        return [a + b for a, b in zip(*totals)]

    def store_split(half, u, rows, value):
        hi, lo = split(value)
        vhi[half, rows, pl.ds(u * TILE, TILE)] = hi
        vlo[half, rows, pl.ds(u * TILE, TILE)] = lo

    for cp in inputs:
        cp.wait_send()
    inputs_in = [
        remote(buf.at[peer_rows], buf.at[peer_rows], insend.at[k], inrecv.at[k], other)
        for k, buf in enumerate((start, site))
    ]
    for cp in inputs_in:
        cp.wait_recv()
    start[my_rows] = init_ref[:, own_cols]
    site[my_rows] = site_ref[:, own_cols]
    masked = live * start[...]
    phases = []
    for u in range(2):
        turned[0, 0, u, own_rows] = masked[:, u * TILE:(u + 1) * TILE]
        phases.append(gather_start(0, u))
    for forward, _ in phases:
        forward()
    for _, finish in phases:
        finish()

    def first_split(half, u, rows):
        value = turned[0, half, u, rows]
        store_split(half, u, rows, value)
        return (value * value,)

    (norm_square,) = over_chunks(first_split, 1)

    for j in range(2):
        local_left[j].wait()
        left_cross[j].wait()
    for q in range(4):
        for k in range(RING):
            hi, lo = split(lstage[q, rows_of(chip(k + 2))])
            lhi[q, pl.ds(k * ROWS, ROWS)] = hi
            llo[q, pl.ds(k * ROWS, ROWS)] = lo

    present = jnp.where(s + 1 < SECTIONS, 1.0, 0.0).astype(F32)

    def diag_arrived(q, piece):
        width = HALF - piece * TILE
        ref = rdiag.at[q, pl.ds(piece * TILE, TILE), pl.ds(piece * TILE, width)]
        remote(ref, ref, rsend.at[0, 0], drecv.at[q, piece], other).wait_recv()

    def off_arrived(q, piece):
        ref = off_piece(q, piece)
        remote(ref, ref, rsend.at[0, 0], brecv.at[q, piece], other).wait_recv()

    def put(q, half, rows, cols, value):
        hi, lo = split(value * present)
        rhi[q, half, rows, cols] = hi
        rlo[q, half, rows, cols] = lo

    low, high = slice(0, TILE), slice(TILE, HALF)

    def prepare(q, u):
        diag_arrived(q, u)
        if u == 0:
            put(q, 0, low, every, rdiag[q, low, :])
            put(q, 0, high, low, rdiag[q, low, high].T)

            @pl.when(c == 0)
            def _():
                put(q, 1, every, low, roff[q, low, :].T)

            @pl.when(c == 1)
            def _():
                put(q, 1, every, low, roff[q, :, low])
        else:
            put(q, 0, high, high, rdiag[q, high, high])

            @pl.when(c == 0)
            def _():
                put(q, 1, every, high, roff[q, high, :].T)

            @pl.when(c == 1)
            def _():
                put(q, 1, every, high, roff[q, :, high])

    subs = (low, high)
    forwards = []
    first_gather = []
    for u in range(2):
        for j in range(2):
            pieces = (0, 1) if u == 0 else (2,)
            for piece in pieces:
                off_arrived(2 * j, piece)
                forwards.append(off_forward(j, piece))
                forwards[-1].start()
            prepare(2 * j, u)
            carry(2 * j, subs[u])
            for piece in pieces:
                off_arrived(2 * j + 1, piece)
            prepare(2 * j + 1, u)
            carry(2 * j + 1, subs[u])
        part[u, far_rows] = bring_back(far_rows, subs[u])
        reduce_far(0, u)
        part[u, near_rows] = bring_back(near_rows, subs[u])
        reduce_near(0, u)
        if u == 1:
            first_gather[0][0]()
        reduce_relay(0, u)
        if u == 1:
            first_gather[0][1]()
        own_image(0, u, turned[0, 0, u, own_rows])
        first_gather.append(gather_start(1, u))
    first_gather[1][0]()
    first_gather[1][1]()
    for cp in shifts + forwards:
        cp.wait_send()
    for u in range(2):
        reduce_sent(0, u)

    inverse = 1.0 / jnp.sqrt(norm_square)

    def first_ritz(half, u, rows):
        est = turned[0, half, u, rows] * inverse
        img = turned[1, half, u, rows] * inverse
        estimate[half, u, rows] = est
        image[half, u, rows] = img
        return (est * img,)

    (ritz,) = over_chunks(first_ritz, 1)

    def first_residual(half, u, rows):
        res = image[half, u, rows] - ritz * estimate[half, u, rows]
        resid[half, u, rows] = res
        store_split(half, u, rows, res)
        return (res * res,)

    (res_square,) = over_chunks(first_residual, 1)

    def coefficients(ritz, res_square, bend):
        half_gap = 0.5 * (bend - ritz)
        radius = jnp.sqrt(half_gap * half_gap + res_square)
        step = -jnp.sqrt(res_square) / (half_gap + radius)
        back = 1.0 / jnp.sqrt(1.0 + step * step)
        return step, back, ritz + half_gap - radius

    def iterate(n, carried):
        ritz, res_square = carried

        def send_far():
            for u in range(2):
                reduce_far(n, u)

        operate(send_far)
        for u in range(2):
            reduce_near(n, u)
        for u in range(2):
            reduce_relay(n, u)
        phases = []
        for u in range(2):
            own_image(n, u, resid[0, u, own_rows])
            phases.append(gather_start(n + 1, u))
        for forward, _ in phases:
            forward()
        for _, finish in phases:
            finish()
        for u in range(2):
            reduce_sent(n, u)
        inverse = 1.0 / jnp.sqrt(res_square)

        def bends(half, u, rows):
            return ((resid[half, u, rows] * inverse) * (turned[n + 1, half, u, rows] * inverse),)

        (bend,) = over_chunks(bends, 1)
        step, back, new_ritz = coefficients(ritz, res_square, bend)
        scaled = step * inverse

        def update(half, u, rows):
            est = (estimate[half, u, rows] + scaled * resid[half, u, rows]) * back
            img = (image[half, u, rows] + scaled * turned[n + 1, half, u, rows]) * back
            estimate[half, u, rows] = est
            image[half, u, rows] = img
            res = img - new_ritz * est
            resid[half, u, rows] = res
            store_split(half, u, rows, res)
            return (res * res,)

        (new_square,) = over_chunks(update, 1)
        return new_ritz, new_square

    ritz, res_square = lax.fori_loop(1, ITERS, iterate, (ritz, res_square))

    operate(None)
    inverse = 1.0 / jnp.sqrt(res_square)
    mine = []
    for u in range(2):
        own = resid[0, u, own_rows] * inverse
        acc = site[:, subs[u]] * own * own
        for k in range(RING):
            acc = acc + (block(u, k)[...] * inverse) * (resid[0, u, rows_of(chip(k))] * inverse)
        mine.append(jnp.sum(acc, axis=(0, 1), keepdims=True))
    mine = mine[0] + mine[1]
    scal[t] = jnp.broadcast_to(mine, (8, 128))
    bends = []
    for k in range(1, 2 * RING):
        cp = remote(scal.at[t], scal.at[t], sc_send.at[k], sc_recv.at[k],
                    (s, lax.rem(t + k, 2 * RING)))
        cp.start()
        bends.append(cp)
    for k in range(1, 2 * RING):
        slot = scal.at[lax.rem(t + 2 * RING - k, 2 * RING)]
        remote(slot, slot, sc_send.at[k], sc_recv.at[k], other).wait_recv()
    bend = jnp.sum(scal[...], axis=0)[0:1, 0:1]
    step, back, ritz = coefficients(ritz, res_square, bend)
    scaled = step * inverse
    out_rows = pl.ds(pl.multiple_of(t * (ROWS // 2), ROWS // 2), ROWS // 2)
    for half, base in ((0, c * HALF), (1, (1 - c) * HALF)):
        for u in range(2):
            est = (estimate[half, u, out_rows] + scaled * resid[half, u, out_rows]) * back
            cols = pl.ds(pl.multiple_of(base + u * TILE, TILE), TILE)
            out_ref[:, cols] = est * (0.5 * PAD)
    energy_ref[0] = ritz[0, 0]
    for cp in bends:
        cp.wait_send()
    for n in range(ITERS + 1):
        for u in range(2):
            gather_sent(n, u)


def per_device(initial, onsite, left_env, right_env, sector_dims):
    vmem = pl.BlockSpec(memory_space=pltpu.VMEM)
    smem = pl.BlockSpec(memory_space=pltpu.SMEM)
    anywhere = pl.BlockSpec(memory_space=pl.ANY)
    dma = pltpu.SemaphoreType.DMA
    full = (2, 2, PAD, TILE)
    return pl.pallas_call(
        kernel,
        out_shape=(
            jax.ShapeDtypeStruct((ROWS // 2, PAD), F32),
            jax.ShapeDtypeStruct((1,), F32),
        ),
        in_specs=[vmem, vmem, anywhere, anywhere, smem],
        out_specs=(vmem, smem),
        scratch_shapes=[
            pltpu.VMEM((4, PAD, PAD), F32),
            pltpu.VMEM((4, PAD, PAD), BF16),
            pltpu.VMEM((4, PAD, PAD), BF16),
            pltpu.VMEM((4, HALF, HALF), F32),
            pltpu.VMEM((4, HALF, HALF), F32),
            pltpu.VMEM((4, 2, HALF, HALF), BF16),
            pltpu.VMEM((4, 2, HALF, HALF), BF16),
            pltpu.VMEM((4, PAD, HALF), BF16),
            pltpu.VMEM((4, PAD, HALF), BF16),
            pltpu.VMEM((ROWS, HALF), F32),
            pltpu.VMEM((ROWS, HALF), F32),
            pltpu.VMEM((ITERS + 1,) + full, F32),
            pltpu.VMEM(full, F32),
            pltpu.VMEM(full, F32),
            pltpu.VMEM(full, F32),
            pltpu.VMEM((2, PAD, HALF), BF16),
            pltpu.VMEM((2, PAD, HALF), BF16),
            pltpu.VMEM((2, PAD, TILE), F32),
            pltpu.VMEM((ITERS, 2, 7, ROWS, TILE), F32),
            pltpu.VMEM((2 * RING, 8, 128), F32),
            dma((2,)), dma((2,)), dma((2,)), dma((2,)), dma((2,)),
            dma((2, 7)), dma((4, 2)), dma((4, 3)), dma((2, 3)),
            dma((ITERS, 2)), dma((ITERS, 2, 7)),
            dma((ITERS + 1, 2)), dma((ITERS + 1, 2, 7)),
            dma((ITERS + 1, 2)), dma((ITERS + 1, 2)),
            dma((2 * RING,)), dma((2 * RING,)),
        ],
        compiler_params=pltpu.CompilerParams(
            collective_id=0, has_side_effects=True, vmem_limit_bytes=56 * 2**20),
        cost_estimate=pl.CostEstimate(
            flops=5 * 3 * 2 * 4 * 2 * PAD * PAD * HALF, bytes_accessed=2**23, transcendentals=0),
    )(initial, onsite, left_env, right_env, sector_dims)


def solution(mesh):
    return jax.shard_map(
        per_device,
        mesh=mesh,
        in_specs=(
            P(("sec", "term"), None),
            P(("sec", "term"), None),
            P("sec", "term", None, None),
            P("sec", "term", None, None),
            P("sec", None),
        ),
        out_specs=(P(("sec", "term"), None), P("sec")),
        check_vma=False,
    )
```

time: 166 us -> 155 us (0.934)
  Pallas kernels: 160 us -> 150 us
    pallas_call x1, Pallas kernels: 160 us -> 150 us  [per_device(): pl.pallas_call(kernel, out_shape=(jax.ShapeDtypeStruct((ROWS // 2, PAD),...]
where the time goes in v2:
time: 155 us; the launch traced here: 154 us
  Pallas kernels  150 us (97%)
  between operations  2.39 us (2%)
    pallas_call x1, Pallas kernels, per_device(): pl.pallas_call(kernel, out_shape=(jax.ShapeDtypeStruct((ROWS // 2, PAD),...  150 us

profile of v2, /device:TPU:30, one launch (start us, length us, event | category | flops | bytes accessed | tf_op | source)
XLA Modules:
  0.0 153.7 jit_solution(14005556876466924390)
XLA Ops:
  0.6 149.9 %shard_map.68 = (f32[32,512]{1,0:T(8,128)}, f32[1]{0:T(128)}) custom-call(f32[32,512]{1,0:T(8,128)} %init_ref.1, f32[32,512]{1,0:T(8,128)} %site_ref.1, f32[1,2,512,512]{3,2,1,0:T(8,128)} %left_ref.1, f32[1,2,512,512]{3,2,1,0:T(8,128)} %right_ref.1, s32[1,2]{1,0:T(1,128)} %dims_ref.1), custom_call_target="tpu_custom_call" | custom-call | flops 16106127360 | bytes 8388608 | tf_op jit(solution)/shard_map/pallas_call | solution.py:512
  150.5 1.5 copy.9

commit v3 on v2

v3 whole, which is shorter than its diff:
```python
import functools

import jax
import jax.numpy as jnp
from jax import lax
from jax.experimental import pallas as pl
from jax.experimental.pallas import tpu as pltpu
from jax.sharding import PartitionSpec as P

ITERS = 4
PAD = 512
HALF = 256
TILE = 128
RING = 8
SECTIONS = 16
ROWS = PAD // RING
MESH = pl.DeviceIdType.MESH
F32, BF16 = jnp.float32, jnp.bfloat16


def dot(a, b):
    return jnp.dot(a, b, preferred_element_type=F32)


def split(x):
    high = x.astype(BF16)
    return high, (x - high.astype(F32)).astype(BF16)


def kernel(
    init_ref, site_ref, left_ref, right_ref, dims_ref, out_ref, energy_ref,
    lstage, lhi, llo, tiles, packed_out, packed, corner, roff, rhi, rlo, chi, clo, cacc,
    start, site, turned, estimate, image, resid, vhi, vlo, part, rsbuf, scal,
    lsem, tsem, lsend, lrecv, insend, inrecv, rsend, psend, precv, drecv, brecv, bfwd,
    rs_send, rs_recv, ag_send, ag_recv, cross_send, cross_recv, sc_send, sc_recv,
):
    s, t = lax.axis_index("sec"), lax.axis_index("term")
    z, c = t // 2, t % 2
    sign = 2 * c - 1

    def chip(k):
        return lax.rem(z + sign * k + 2 * RING, RING)

    def on_ring(k):
        return (s, chip(k) * 2 + c)

    other = (s, z * 2 + 1 - c)
    before = lax.rem(s + SECTIONS - 1, SECTIONS)
    after = lax.rem(s + 1, SECTIONS)

    def rows_of(chip_index):
        return pl.ds(pl.multiple_of(chip_index * ROWS, ROWS), ROWS)

    def remote(src, dst, send, recv, to):
        return pltpu.make_async_remote_copy(
            src_ref=src, dst_ref=dst, send_sem=send, recv_sem=recv,
            device_id=to, device_id_type=MESH,
        )

    local_left = [
        pltpu.make_async_copy(left_ref.at[0, j], lstage.at[2 * j], lsem.at[j])
        for j in range(2)
    ]
    for cp in local_left:
        cp.start()

    def tile_copy(j, kind, u):
        base = pl.multiple_of((c if kind == 0 else 1 - c) * HALF + u * TILE, TILE)
        return pltpu.make_async_copy(
            right_ref.at[0, j, pl.ds(base, TILE), pl.ds(base, TILE)],
            tiles.at[j, kind, u], tsem.at[j, kind, u])

    for u in range(2):
        for kind in range(2):
            for j in range(2):
                tile_copy(j, kind, u).start()

    barrier = pltpu.get_barrier_semaphore()
    greeted = [on_ring(k) for k in (1, -1, 2, -2)] + [other]
    greeted += [(after, z * 2 + k) for k in range(2)]
    for device in greeted:
        pl.semaphore_signal(barrier, inc=1, device_id=device, device_id_type=MESH)
    pl.semaphore_wait(barrier, len(greeted))

    own_cols = pl.ds(pl.multiple_of(c * HALF, HALF), HALF)
    other_cols = pl.ds(pl.multiple_of((1 - c) * HALF, HALF), HALF)
    my_rows = pl.ds(pl.multiple_of(c * (ROWS // 2), ROWS // 2), ROWS // 2)
    peer_rows = pl.ds(pl.multiple_of((1 - c) * (ROWS // 2), ROWS // 2), ROWS // 2)
    inputs = [
        remote(ref.at[:, other_cols], buf.at[my_rows], insend.at[k], inrecv.at[k], other)
        for k, (ref, buf) in enumerate(((init_ref, start), (site_ref, site)))
    ]
    for cp in inputs:
        cp.start()

    def target(kind):
        return (before, z * 2 + (c if kind == 0 else 1 - c))

    def corner_copy(j, kind):
        base = (c if kind == 0 else 1 - c) * HALF
        return remote(
            right_ref.at[0, j, pl.ds(pl.multiple_of(base, TILE), TILE),
                         pl.ds(pl.multiple_of(base + TILE, TILE), TILE)],
            corner.at[2 * j + kind], rsend.at[j, kind], drecv.at[2 * j + kind], target(kind))

    off_parts = ((0, 0, HALF), (TILE, 0, TILE), (TILE, TILE, TILE))

    def off_piece(slot, piece):
        r0, c0, width = off_parts[piece]
        return roff.at[slot, pl.ds(r0, TILE), pl.ds(c0, width)]

    def off_copy(j, piece):
        r0, c0, width = off_parts[piece]
        return remote(
            right_ref.at[0, j, pl.ds(r0, TILE), pl.ds(HALF + c0, width)],
            off_piece(2 * j, piece), rsend.at[j, 2 + piece], brecv.at[2 * j, piece],
            (before, t))

    def off_forward(j, piece):
        return remote(off_piece(2 * j, piece), off_piece(2 * j + 1, piece),
                      bfwd.at[j, piece], brecv.at[2 * j + 1, piece], other)

    def packed_copy(kind, u):
        return remote(packed_out.at[kind, u], packed.at[kind, u],
                      psend.at[kind, u], precv.at[kind, u], target(kind))

    tile_row = lax.broadcasted_iota(jnp.int32, (TILE, TILE), 0)
    tile_col = lax.broadcasted_iota(jnp.int32, (TILE, TILE), 1)

    def pack(kind, u):
        for j in range(2):
            tile_copy(j, kind, u).wait()
        second = tiles[1, kind, u]
        packed_out[kind, u, pl.ds(0, TILE)] = jnp.where(
            tile_row <= tile_col, tiles[0, kind, u], second)
        line = jnp.sum(jnp.where(tile_row == tile_col, second, 0.0), axis=0, keepdims=True)
        packed_out[kind, u, pl.ds(TILE, 8)] = jnp.broadcast_to(line, (8, TILE))

    def unpack(kind, u):
        both = packed[kind, u, pl.ds(0, TILE)]
        line = packed[kind, u, pl.ds(TILE, 8)][0:1]
        mirrored = both.T
        first = jnp.where(tile_row <= tile_col, both, mirrored)
        second = jnp.where(tile_row > tile_col, both, mirrored)
        return first, jnp.where(tile_row == tile_col, line, second)

    shifts = [off_copy(0, 0), off_copy(0, 1), corner_copy(0, 0), corner_copy(0, 1)]
    for cp in shifts:
        cp.start()
    for u in range(2):
        for kind in range(2):
            pack(kind, u)
    later = [packed_copy(0, 0), packed_copy(1, 0)]
    later += [off_copy(1, 0), off_copy(1, 1), corner_copy(1, 0), corner_copy(1, 1)]
    later += [packed_copy(0, 1), packed_copy(1, 1), off_copy(0, 2), off_copy(1, 2)]
    for cp in later:
        cp.start()
    shifts += later
    left_cross = [
        remote(left_ref.at[0, j], lstage.at[2 * j + 1], lsend.at[j], lrecv.at[j], other)
        for j in range(2)
    ]
    for cp in left_cross:
        cp.start()

    row_index = lax.broadcasted_iota(jnp.int32, (ROWS, HALF), 0) + z * ROWS
    col_index = lax.broadcasted_iota(jnp.int32, (ROWS, HALF), 1) + c * HALF
    live = jnp.where(
        (row_index < dims_ref[0, 0]) & (col_index < dims_ref[0, 1]), 1.0, 0.0).astype(F32)

    own_rows = rows_of(z)

    def gather_start(n, u):
        def ring_copy(k, src_chip, index):
            piece = turned.at[n, 0, u, rows_of(src_chip)]
            return remote(piece, piece, ag_send.at[n, u], ag_recv.at[n, u, index], on_ring(k))

        def cross(k):
            rows = rows_of(chip(k))
            remote(turned.at[n, 0, u, rows], turned.at[n, 1, u, rows],
                   cross_send.at[n, u], cross_recv.at[n, u], other).start()

        def received(index, k):
            piece = turned.at[n, 0, u, rows_of(chip(k))]
            remote(piece, piece, ag_send.at[n, u], ag_recv.at[n, u, index],
                   on_ring(k)).wait_recv()

        ring_copy(2, z, 0).start()
        ring_copy(-2, z, 1).start()
        ring_copy(1, z, 2).start()
        ring_copy(-1, z, 3).start()
        cross(0)

        def forward():
            received(0, -2)
            ring_copy(2, chip(-2), 5).start()
            ring_copy(1, chip(-2), 4).start()
            received(1, 2)
            ring_copy(-1, chip(2), 6).start()
            cross(-2)
            cross(2)
            received(2, -1)
            cross(-1)
            received(3, 1)
            cross(1)

        def finish():
            received(4, -3)
            cross(-3)
            received(6, 3)
            cross(3)
            received(5, -4)
            cross(-4)

        def complete():
            other_half = turned.at[n, 1, u]
            remote(other_half, other_half, cross_send.at[n, u], cross_recv.at[n, u],
                   other).wait_recv()

        return forward, finish, complete

    def gather_sent(n, u):
        seven = rsbuf.at[0, 0]
        remote(seven, seven, ag_send.at[n, u], ag_recv.at[n, u, 0], other).wait_send()
        half = turned.at[n, 0, u]
        remote(half, half, cross_send.at[n, u], cross_recv.at[n, u], other).wait_send()

    def block(u, j):
        return part.at[u, pl.ds((j + 6) % RING * ROWS, ROWS)]

    def reduce_send(n, u, src, slot, k):
        remote(src, rsbuf.at[n, u, slot], rs_send.at[n, u], rs_recv.at[n, u, slot],
               on_ring(k)).start()

    def reduce_wait(n, u, slot):
        piece = rsbuf.at[n, u, slot]
        remote(piece, piece, rs_send.at[n, u], rs_recv.at[n, u, slot], on_ring(1)).wait_recv()

    def reduce_far(n, u):
        reduce_send(n, u, block(u, 4), 1, 2)
        reduce_send(n, u, block(u, 3), 0, 1)
        reduce_send(n, u, block(u, 5), 2, -1)

    def reduce_near(n, u):
        reduce_send(n, u, block(u, 1), 3, 1)
        reduce_send(n, u, block(u, 7), 4, -1)

    def reduce_relay(n, u):
        reduce_wait(n, u, 0)
        reduce_wait(n, u, 1)
        block(u, 2)[...] = block(u, 2)[...] + rsbuf[n, u, 0] + rsbuf[n, u, 1]
        reduce_send(n, u, block(u, 2), 5, 2)
        reduce_wait(n, u, 2)
        block(u, 6)[...] = block(u, 6)[...] + rsbuf[n, u, 2]
        reduce_send(n, u, block(u, 6), 6, -2)

    def reduce_final(n, u):
        reduce_wait(n, u, 3)
        reduce_wait(n, u, 4)
        total = block(u, 0)[...] + rsbuf[n, u, 3] + rsbuf[n, u, 4]
        reduce_wait(n, u, 5)
        reduce_wait(n, u, 6)
        return total + rsbuf[n, u, 5] + rsbuf[n, u, 6]

    def reduce_sent(n, u):
        seven = rsbuf.at[n, u]
        remote(seven, seven, rs_send.at[n, u], rs_recv.at[n, u, 0], other).wait_send()

    def own_image(n, u, vector):
        cols = slice(u * TILE, (u + 1) * TILE)
        turned[n + 1, 0, u, own_rows] = live[:, cols] * (
            reduce_final(n, u) + site[:, cols] * vector)

    def carry(q, u):
        cols = slice(u * TILE, (u + 1) * TILE)
        acc = None
        for k in range(2):
            new = (dot(vhi[k], rhi[q, k, :, cols]) + dot(vlo[k], rhi[q, k, :, cols])
                   + dot(vhi[k], rlo[q, k, :, cols]))
            acc = new if acc is None else acc + new
        chi[q, :, cols], clo[q, :, cols] = split(acc)

    def carry_part(q, k):
        return dot(vhi[k], rhi[q, k]) + dot(vlo[k], rhi[q, k]) + dot(vhi[k], rlo[q, k])

    def bring_back(rows, cols):
        terms = [
            dot(lhi[q, rows], chi[q, :, cols]) + dot(llo[q, rows], chi[q, :, cols])
            + dot(lhi[q, rows], clo[q, :, cols])
            for q in range(4)
        ]
        return (terms[0] + terms[1]) + (terms[2] + terms[3])

    far_rows, near_rows = slice(0, HALF), slice(HALF, PAD)
    every = slice(0, HALF)

    def products(u):
        cols = slice(u * TILE, (u + 1) * TILE)
        part[u, far_rows] = bring_back(far_rows, cols)
        reduce_far(0, u)
        part[u, near_rows] = bring_back(near_rows, cols)
        reduce_near(0, u)

    def operate(after_far):
        for rows, then in ((far_rows, after_far), (near_rows, None)):
            fresh = bring_back(rows, every)
            for u in range(2):
                part[u, rows] = fresh[:, u * TILE:(u + 1) * TILE]
            if then is not None:
                then()

    CHUNK = 128

    def over_chunks(body, u):
        totals = []
        for half in range(2):
            def step(i, acc, half=half):
                value = body(half, u, pl.ds(pl.multiple_of(i * CHUNK, CHUNK), CHUNK))
                return acc + jnp.sum(value.reshape(CHUNK // 8, 8, TILE), axis=0)
            acc = lax.fori_loop(0, PAD // CHUNK, step, jnp.zeros((8, TILE), F32))
            totals.append(jnp.sum(acc, axis=(0, 1), keepdims=True))
        return totals

    def combine(first, second):
        return (first[0] + second[0]) + (first[1] + second[1])

    def store_split(half, u, rows, value):
        hi, lo = split(value)
        vhi[u, rows, pl.ds(half * TILE, TILE)] = hi
        vlo[u, rows, pl.ds(half * TILE, TILE)] = lo

    def bend_part(u, inverse):
        own = resid[0, u, own_rows] * inverse
        acc = site[:, u * TILE:(u + 1) * TILE] * own * own
        for k in range(RING):
            acc = acc + (block(u, k)[...] * inverse) * (
                resid[0, u, rows_of(chip(k))] * inverse)
        return jnp.sum(acc, axis=(0, 1), keepdims=True)

    def send_bend(n, mine):
        scal[n, t] = jnp.broadcast_to(mine, (1, TILE))
        for k in range(1, 2 * RING):
            remote(scal.at[n, t], scal.at[n, t], sc_send.at[n], sc_recv.at[n],
                   (s, lax.rem(t + k, 2 * RING))).start()

    def bend_total(n):
        others = scal.at[n, pl.ds(0, 2 * RING - 1)]
        remote(others, others, sc_send.at[n], sc_recv.at[n], other).wait()
        return jnp.sum(scal[n], axis=0)[:, 0:1]

    def coefficients(ritz, res_square, bend):
        half_gap = 0.5 * (bend - ritz)
        radius = jnp.sqrt(half_gap * half_gap + res_square)
        step = -jnp.sqrt(res_square) / (half_gap + radius)
        back = 1.0 / jnp.sqrt(1.0 + step * step)
        return step, back, ritz + half_gap - radius

    def absorb(n, u, scaled, back, ritz):
        def update(half, u, rows):
            est = (estimate[half, u, rows] + scaled * resid[half, u, rows]) * back
            img = (image[half, u, rows] + scaled * turned[n + 1, half, u, rows]) * back
            estimate[half, u, rows] = est
            image[half, u, rows] = img
            res = img - ritz * est
            resid[half, u, rows] = res
            store_split(half, u, rows, res)
            return res * res

        sums = over_chunks(update, u)
        for q in range(4):
            if u == 0:
                cacc[q] = carry_part(q, 0)
            else:
                chi[q], clo[q] = split(cacc[q] + carry_part(q, 1))
        return sums

    def take_in(n, phases, scaled, back, ritz):
        phases[0][1]()
        phases[0][2]()
        first = absorb(n, 0, scaled, back, ritz)
        phases[1][1]()
        phases[1][2]()
        second = absorb(n, 1, scaled, back, ritz)
        return combine(first, second)

    for cp in inputs:
        cp.wait_send()
    inputs_in = [
        remote(buf.at[peer_rows], buf.at[peer_rows], insend.at[k], inrecv.at[k], other)
        for k, buf in enumerate((start, site))
    ]
    for cp in inputs_in:
        cp.wait_recv()
    start[my_rows] = init_ref[:, own_cols]
    site[my_rows] = site_ref[:, own_cols]
    masked = live * start[...]
    phases = []
    for u in range(2):
        turned[0, 0, u, own_rows] = masked[:, u * TILE:(u + 1) * TILE]
        phases.append(gather_start(0, u))
    for forward, _, _ in phases:
        forward()
    for _, finish, complete in phases:
        finish()
        complete()

    def first_split(half, u, rows):
        value = turned[0, half, u, rows]
        zero = jnp.zeros_like(value)
        resid[half, u, rows] = value
        estimate[half, u, rows] = zero
        image[half, u, rows] = zero
        store_split(half, u, rows, value)
        return value * value

    norm_square = combine(over_chunks(first_split, 0), over_chunks(first_split, 1))

    for j in range(2):
        local_left[j].wait()
        left_cross[j].wait()
    for q in range(4):
        for k in range(RING):
            hi, lo = split(lstage[q, rows_of(chip(k + 2))])
            lhi[q, pl.ds(k * ROWS, ROWS)] = hi
            llo[q, pl.ds(k * ROWS, ROWS)] = lo

    present = jnp.where(s + 1 < SECTIONS, 1.0, 0.0).astype(F32)

    def arrived(ref, sem):
        remote(ref, ref, rsend.at[0, 0], sem, other).wait_recv()

    def put(q, k, half, u, value):
        hi, lo = split(value * present)
        rows, cols = pl.ds(half * TILE, TILE), pl.ds(u * TILE, TILE)
        rhi[q, k, rows, cols] = hi
        rlo[q, k, rows, cols] = lo

    def put_off(q, u):
        for k in range(2):
            @pl.when(c == 0)
            def _():
                put(q, k, 1, u, roff[q, pl.ds(u * TILE, TILE), pl.ds(k * TILE, TILE)].T)

            @pl.when(c == 1)
            def _():
                put(q, k, 1, u, roff[q, pl.ds(k * TILE, TILE), pl.ds(u * TILE, TILE)])

    def put_diag(u):
        for kind in range(2):
            arrived(packed.at[kind, u], precv.at[kind, u])
            for j, value in enumerate(unpack(kind, u)):
                put(2 * j + kind, u, 0, u, value)

    forwards = []

    def off_arrived(j, u):
        for piece in ((0, 1) if u == 0 else (2,)):
            arrived(off_piece(2 * j, piece), brecv.at[2 * j, piece])
            forwards.append(off_forward(j, piece))
            forwards[-1].start()

    def first_carry(j, u):
        for q in (2 * j, 2 * j + 1):
            if q % 2:
                for piece in ((0, 1) if u == 0 else (2,)):
                    arrived(off_piece(q, piece), brecv.at[q, piece])
            put_off(q, u)
            if u == 0:
                arrived(corner.at[q], drecv.at[q])
                put(q, 0, 0, 1, corner[q])
                put(q, 1, 0, 0, corner[q].T)
            carry(q, u)

    off_arrived(0, 0)
    put_diag(0)
    first_carry(0, 0)
    off_arrived(1, 0)
    first_carry(1, 0)
    products(0)
    inverse = 1.0 / jnp.sqrt(norm_square)
    bend_share = bend_part(0, inverse)
    off_arrived(0, 1)
    put_diag(1)
    first_carry(0, 1)
    reduce_relay(0, 0)
    off_arrived(1, 1)
    first_carry(1, 1)
    own_image(0, 0, resid[0, 0, own_rows])
    phases = [gather_start(1, 0)]
    products(1)
    send_bend(0, bend_share + bend_part(1, inverse))
    phases[0][0]()
    reduce_relay(0, 1)
    own_image(0, 1, resid[0, 1, own_rows])
    phases.append(gather_start(1, 1))
    ritz = bend_total(0)
    phases[1][0]()
    res_square = take_in(0, phases, inverse, 1.0, ritz)
    for cp in shifts + forwards:
        cp.wait_send()
    for u in range(2):
        reduce_sent(0, u)

    def iterate(n, carried):
        ritz, res_square = carried
        inverse = 1.0 / jnp.sqrt(res_square)

        def send_far():
            for u in range(2):
                reduce_far(n, u)

        operate(send_far)
        for u in range(2):
            reduce_near(n, u)
        send_bend(n, bend_part(0, inverse) + bend_part(1, inverse))
        for u in range(2):
            reduce_relay(n, u)
        phases = []
        for u in range(2):
            own_image(n, u, resid[0, u, own_rows])
            phases.append(gather_start(n + 1, u))
        step, back, new_ritz = coefficients(ritz, res_square, bend_total(n))
        for forward, _, _ in phases:
            forward()
        new_square = take_in(n, phases, step * inverse, back, new_ritz)
        for u in range(2):
            reduce_sent(n, u)
        return new_ritz, new_square

    ritz, res_square = lax.fori_loop(1, ITERS, iterate, (ritz, res_square))

    operate(None)
    inverse = 1.0 / jnp.sqrt(res_square)
    send_bend(ITERS, bend_part(0, inverse) + bend_part(1, inverse))
    step, back, ritz = coefficients(ritz, res_square, bend_total(ITERS))
    scaled = step * inverse
    out_rows = pl.ds(pl.multiple_of(t * (ROWS // 2), ROWS // 2), ROWS // 2)
    for half, base in ((0, c * HALF), (1, (1 - c) * HALF)):
        for u in range(2):
            est = (estimate[half, u, out_rows] + scaled * resid[half, u, out_rows]) * back
            cols = pl.ds(pl.multiple_of(base + u * TILE, TILE), TILE)
            out_ref[:, cols] = est * (0.5 * PAD)
    energy_ref[0] = ritz[0, 0]
    for n in range(ITERS + 1):
        for u in range(2):
            gather_sent(n, u)


def per_device(initial, onsite, left_env, right_env, sector_dims):
    vmem = pl.BlockSpec(memory_space=pltpu.VMEM)
    smem = pl.BlockSpec(memory_space=pltpu.SMEM)
    anywhere = pl.BlockSpec(memory_space=pl.ANY)
    dma = pltpu.SemaphoreType.DMA
    full = (2, 2, PAD, TILE)
    return pl.pallas_call(
        kernel,
        out_shape=(
            jax.ShapeDtypeStruct((ROWS // 2, PAD), F32),
            jax.ShapeDtypeStruct((1,), F32),
        ),
        in_specs=[vmem, vmem, anywhere, anywhere, smem],
        out_specs=(vmem, smem),
        scratch_shapes=[
            pltpu.VMEM((4, PAD, PAD), F32),
            pltpu.VMEM((4, PAD, PAD), BF16),
            pltpu.VMEM((4, PAD, PAD), BF16),
            pltpu.VMEM((2, 2, 2, TILE, TILE), F32),
            pltpu.VMEM((2, 2, TILE + 8, TILE), F32),
            pltpu.VMEM((2, 2, TILE + 8, TILE), F32),
            pltpu.VMEM((4, TILE, TILE), F32),
            pltpu.VMEM((4, HALF, HALF), F32),
            pltpu.VMEM((4, 2, HALF, HALF), BF16),
            pltpu.VMEM((4, 2, HALF, HALF), BF16),
            pltpu.VMEM((4, PAD, HALF), BF16),
            pltpu.VMEM((4, PAD, HALF), BF16),
            pltpu.VMEM((4, PAD, HALF), F32),
            pltpu.VMEM((ROWS, HALF), F32),
            pltpu.VMEM((ROWS, HALF), F32),
            pltpu.VMEM((ITERS + 1,) + full, F32),
            pltpu.VMEM(full, F32),
            pltpu.VMEM(full, F32),
            pltpu.VMEM(full, F32),
            pltpu.VMEM((2, PAD, HALF), BF16),
            pltpu.VMEM((2, PAD, HALF), BF16),
            pltpu.VMEM((2, PAD, TILE), F32),
            pltpu.VMEM((ITERS, 2, 7, ROWS, TILE), F32),
            pltpu.VMEM((ITERS + 1, 2 * RING, 1, TILE), F32),
            dma((2,)), dma((2, 2, 2)), dma((2,)), dma((2,)), dma((2,)), dma((2,)),
            dma((2, 5)), dma((2, 2)), dma((2, 2)), dma((4,)), dma((4, 3)), dma((2, 3)),
            dma((ITERS, 2)), dma((ITERS, 2, 7)),
            dma((ITERS + 1, 2)), dma((ITERS + 1, 2, 7)),
            dma((ITERS + 1, 2)), dma((ITERS + 1, 2)),
            dma((ITERS + 1,)), dma((ITERS + 1,)),
        ],
        compiler_params=pltpu.CompilerParams(
            collective_id=0, has_side_effects=True, vmem_limit_bytes=56 * 2**20),
        cost_estimate=pl.CostEstimate(
            flops=5 * 3 * 2 * 4 * 2 * PAD * PAD * HALF, bytes_accessed=2**23, transcendentals=0),
    )(initial, onsite, left_env, right_env, sector_dims)


def solution(mesh):
    return jax.shard_map(
        per_device,
        mesh=mesh,
        in_specs=(
            P(("sec", "term"), None),
            P(("sec", "term"), None),
            P("sec", "term", None, None),
            P("sec", "term", None, None),
            P("sec", None),
        ),
        out_specs=(P(("sec", "term"), None), P("sec")),
        check_vma=False,
    )
```

time: 155 us -> 146 us (0.942)
  Pallas kernels: 150 us -> 142 us
    pallas_call x1, Pallas kernels: 150 us -> 142 us  [per_device(): pl.pallas_call(kernel, out_shape=(jax.ShapeDtypeStruct((ROWS // 2, PAD),...]
where the time goes in v3:
time: 146 us
  Pallas kernels  142 us (97%)
  between operations  2.39 us (2%)
  local copies, waits for them, and re-layouts  1.47 us (1%)
    pallas_call x1, Pallas kernels, per_device(): pl.pallas_call(kernel, out_shape=(jax.ShapeDtypeStruct((ROWS // 2, PAD),...  142 us

profile of v3, /device:TPU:30, one launch (start us, length us, event | category | flops | bytes accessed | tf_op | source)
XLA Modules:
  0.0 146.3 jit_solution(12792098516140340932)
XLA Ops:
  0.6 142.4 %shard_map.68 = (f32[32,512]{1,0:T(8,128)}, f32[1]{0:T(128)}) custom-call(f32[32,512]{1,0:T(8,128)} %init_ref.1, f32[32,512]{1,0:T(8,128)} %site_ref.1, f32[1,2,512,512]{3,2,1,0:T(8,128)} %left_ref.1, f32[1,2,512,512]{3,2,1,0:T(8,128)} %right_ref.1, s32[1,2]{1,0:T(1,128)} %dims_ref.1), custom_call_target="tpu_custom_call" | custom-call | flops 16106127360 | bytes 8388608 | tf_op jit(solution)/shard_map/pallas_call | solution.py:555
  143.0 1.5 %copy.9 = f32[32,512]{1,0:T(8,128)} copy(f32[32,512]{1,0:T(8,128)} %get-tuple-element.4) | data formatting | bytes 131072

commit v4 on v3

--- a/solution.py
+++ b/solution.py
@@ -13,6 +13,9 @@
 TILE = 128
 RING = 8
 SECTIONS = 16
+GROUPS = ((0, -1, 1, -2, 2), (-3, 3, 4))
+LONG_WAY = 3
+SIDE = 4
 ROWS = PAD // RING
 MESH = pl.DeviceIdType.MESH
 F32, BF16 = jnp.float32, jnp.bfloat16
@@ -29,9 +32,9 @@
 
 def kernel(
     init_ref, site_ref, left_ref, right_ref, dims_ref, out_ref, energy_ref,
-    lstage, lhi, llo, tiles, packed_out, packed, corner, roff, rhi, rlo, chi, clo, cacc,
+    lstage, lhi, llo, tiles, packed_out, packed, corner, roff, rhi, rlo, chi, clo, squares, passing,
     start, site, turned, estimate, image, resid, vhi, vlo, part, rsbuf, scal,
-    lsem, tsem, lsend, lrecv, insend, inrecv, rsend, psend, precv, drecv, brecv, bfwd,
+    lsem, tsem, lsend, lrecv, insend, inrecv, rsend, psend, precv, drecv, brecv, bfwd, hsend, hrecv,
     rs_send, rs_recv, ag_send, ag_recv, cross_send, cross_recv, sc_send, sc_recv,
 ):
     s, t = lax.axis_index("sec"), lax.axis_index("term")
@@ -47,6 +50,14 @@
     other = (s, z * 2 + 1 - c)
     before = lax.rem(s + SECTIONS - 1, SECTIONS)
     after = lax.rem(s + 1, SECTIONS)
+    x, y = s % SIDE, s // SIDE
+
+    def section_at(x_of, y_of):
+        return lax.rem(y_of + SIDE, SIDE) * SIDE + lax.rem(x_of + SIDE, SIDE)
+
+    right, left = section_at(x + 1, y), section_at(x - 1, y)
+    last_to = section_at(x + 1, y - (x == SIDE - 2).astype(jnp.int32))
+    last_from = section_at(x - 1, y + (x == SIDE - 1).astype(jnp.int32))
 
     def rows_of(chip_index):
         return pl.ds(pl.multiple_of(chip_index * ROWS, ROWS), ROWS)
@@ -77,9 +88,33 @@
 
     barrier = pltpu.get_barrier_semaphore()
     greeted = [on_ring(k) for k in (1, -1, 2, -2)] + [other]
-    greeted += [(after, z * 2 + k) for k in range(2)]
+    greeted += [(after, z * 2 + k) for k in range(2)] + [(left, t), (last_from, t)]
     for device in greeted:
         pl.semaphore_signal(barrier, inc=1, device_id=device, device_id_type=MESH)
+    tile_row = lax.broadcasted_iota(jnp.int32, (TILE, TILE), 0)
+    tile_col = lax.broadcasted_iota(jnp.int32, (TILE, TILE), 1)
+
+    def pack(kind, u):
+        for j in range(2):
+            tile_copy(j, kind, u).wait()
+        second = tiles[1, kind, u]
+        packed_out[kind, u, pl.ds(0, TILE)] = jnp.where(
+            tile_row <= tile_col, tiles[0, kind, u], second)
+        line = jnp.sum(jnp.where(tile_row == tile_col, second, 0.0), axis=0, keepdims=True)
+        packed_out[kind, u, pl.ds(TILE, 8)] = jnp.broadcast_to(line, (8, TILE))
+
+    def split_left(q):
+        for k in range(RING):
+            hi, lo = split(lstage[q, rows_of(chip(k + 2))])
+            lhi[q, pl.ds(k * ROWS, ROWS)] = hi
+            llo[q, pl.ds(k * ROWS, ROWS)] = lo
+
+    for u in range(2):
+        for kind in range(2):
+            pack(kind, u)
+    for j in range(2):
+        local_left[j].wait()
+        split_left(2 * j)
     pl.semaphore_wait(barrier, len(greeted))
 
     own_cols = pl.ds(pl.multiple_of(c * HALF, HALF), HALF)
@@ -111,10 +146,26 @@
 
     def off_copy(j, piece):
         r0, c0, width = off_parts[piece]
-        return remote(
-            right_ref.at[0, j, pl.ds(r0, TILE), pl.ds(HALF + c0, width)],
-            off_piece(2 * j, piece), rsend.at[j, 2 + piece], brecv.at[2 * j, piece],
-            (before, t))
+        src = right_ref.at[0, j, pl.ds(r0, TILE), pl.ds(HALF + c0, width)]
+        i = 2 * (piece - 1) + j
+        if piece == 0 or i >= LONG_WAY:
+            return remote(src, off_piece(2 * j, piece), rsend.at[j, 2 + (piece > 0)],
+                          brecv.at[2 * j, piece], (before, t))
+        return remote(src, passing.at[0, i], hsend.at[0, i], hrecv.at[0, i], (right, t))
+
+    passed = []
+
+    def pass_on(hop, i):
+        src = passing.at[hop, i]
+        remote(src, src, hsend.at[hop, i], hrecv.at[hop, i], other).wait_recv()
+        if hop == 0:
+            cp = remote(src, passing.at[1, i], hsend.at[1, i], hrecv.at[1, i], (right, t))
+        else:
+            j, piece = i % 2, 1 + i // 2
+            cp = remote(src, off_piece(2 * j, piece), hsend.at[2, i], brecv.at[2 * j, piece],
+                        (last_to, t))
+        cp.start()
+        passed.append(cp)
 
     def off_forward(j, piece):
         return remote(off_piece(2 * j, piece), off_piece(2 * j + 1, piece),
@@ -123,18 +174,6 @@
     def packed_copy(kind, u):
         return remote(packed_out.at[kind, u], packed.at[kind, u],
                       psend.at[kind, u], precv.at[kind, u], target(kind))
-
-    tile_row = lax.broadcasted_iota(jnp.int32, (TILE, TILE), 0)
-    tile_col = lax.broadcasted_iota(jnp.int32, (TILE, TILE), 1)
-
-    def pack(kind, u):
-        for j in range(2):
-            tile_copy(j, kind, u).wait()
-        second = tiles[1, kind, u]
-        packed_out[kind, u, pl.ds(0, TILE)] = jnp.where(
-            tile_row <= tile_col, tiles[0, kind, u], second)
-        line = jnp.sum(jnp.where(tile_row == tile_col, second, 0.0), axis=0, keepdims=True)
-        packed_out[kind, u, pl.ds(TILE, 8)] = jnp.broadcast_to(line, (8, TILE))
 
     def unpack(kind, u):
         both = packed[kind, u, pl.ds(0, TILE)]
@@ -144,18 +183,13 @@
         second = jnp.where(tile_row > tile_col, both, mirrored)
         return first, jnp.where(tile_row == tile_col, line, second)
 
-    shifts = [off_copy(0, 0), off_copy(0, 1), corner_copy(0, 0), corner_copy(0, 1)]
+    shifts = [off_copy(0, 1), off_copy(1, 1), off_copy(0, 2)]
+    shifts += [off_copy(0, 0), corner_copy(0, 0), corner_copy(0, 1)]
+    shifts += [packed_copy(0, 0), packed_copy(1, 0)]
+    shifts += [off_copy(1, 0), corner_copy(1, 0), corner_copy(1, 1)]
+    shifts += [packed_copy(0, 1), packed_copy(1, 1), off_copy(1, 2)]
     for cp in shifts:
         cp.start()
-    for u in range(2):
-        for kind in range(2):
-            pack(kind, u)
-    later = [packed_copy(0, 0), packed_copy(1, 0)]
-    later += [off_copy(1, 0), off_copy(1, 1), corner_copy(1, 0), corner_copy(1, 1)]
-    later += [packed_copy(0, 1), packed_copy(1, 1), off_copy(0, 2), off_copy(1, 2)]
-    for cp in later:
-        cp.start()
-    shifts += later
     left_cross = [
         remote(left_ref.at[0, j], lstage.at[2 * j + 1], lsend.at[j], lrecv.at[j], other)
         for j in range(2)
@@ -177,8 +211,9 @@
 
         def cross(k):
             rows = rows_of(chip(k))
+            group = 0 if abs(k) <= 2 else 1
             remote(turned.at[n, 0, u, rows], turned.at[n, 1, u, rows],
-                   cross_send.at[n, u], cross_recv.at[n, u], other).start()
+                   cross_send.at[n, u], cross_recv.at[n, u, group], other).start()
 
         def received(index, k):
             piece = turned.at[n, 0, u, rows_of(chip(k))]
@@ -212,9 +247,9 @@
             received(5, -4)
             cross(-4)
 
-        def complete():
-            other_half = turned.at[n, 1, u]
-            remote(other_half, other_half, cross_send.at[n, u], cross_recv.at[n, u],
+        def complete(group):
+            some = turned.at[n, 1, u, pl.ds(0, len(GROUPS[group]) * ROWS)]
+            remote(some, some, cross_send.at[n, u], cross_recv.at[n, u, group],
                    other).wait_recv()
 
         return forward, finish, complete
@@ -223,7 +258,7 @@
         seven = rsbuf.at[0, 0]
         remote(seven, seven, ag_send.at[n, u], ag_recv.at[n, u, 0], other).wait_send()
         half = turned.at[n, 0, u]
-        remote(half, half, cross_send.at[n, u], cross_recv.at[n, u], other).wait_send()
+        remote(half, half, cross_send.at[n, u], cross_recv.at[n, u, 0], other).wait_send()
 
     def block(u, j):
         return part.at[u, pl.ds((j + 6) % RING * ROWS, ROWS)]
@@ -280,8 +315,18 @@
             acc = new if acc is None else acc + new
         chi[q, :, cols], clo[q, :, cols] = split(acc)
 
-    def carry_part(q, k):
-        return dot(vhi[k], rhi[q, k]) + dot(vlo[k], rhi[q, k]) + dot(vhi[k], rlo[q, k])
+    def carry_rows(group):
+        where = [rows_of(chip(k)) for k in GROUPS[group]]
+        high = [jnp.concatenate([vhi[k, rows] for rows in where], axis=0) for k in range(2)]
+        low = [jnp.concatenate([vlo[k, rows] for rows in where], axis=0) for k in range(2)]
+        for q in range(4):
+            acc = (dot(high[0], rhi[q, 0]) + dot(high[1], rhi[q, 1])
+                   + dot(low[0], rhi[q, 0]) + dot(low[1], rhi[q, 1])
+                   + dot(high[0], rlo[q, 0]) + dot(high[1], rlo[q, 1]))
+            hi, lo = split(acc)
+            for i, rows in enumerate(where):
+                chi[q, rows] = hi[i * ROWS:(i + 1) * ROWS]
+                clo[q, rows] = lo[i * ROWS:(i + 1) * ROWS]
 
     def bring_back(rows, cols):
         terms = [
@@ -355,33 +400,37 @@
         back = 1.0 / jnp.sqrt(1.0 + step * step)
         return step, back, ritz + half_gap - radius
 
-    def absorb(n, u, scaled, back, ritz):
-        def update(half, u, rows):
-            est = (estimate[half, u, rows] + scaled * resid[half, u, rows]) * back
-            img = (image[half, u, rows] + scaled * turned[n + 1, half, u, rows]) * back
-            estimate[half, u, rows] = est
-            image[half, u, rows] = img
-            res = img - ritz * est
-            resid[half, u, rows] = res
-            store_split(half, u, rows, res)
-            return res * res
-
-        sums = over_chunks(update, u)
-        for q in range(4):
-            if u == 0:
-                cacc[q] = carry_part(q, 0)
-            else:
-                chi[q], clo[q] = split(cacc[q] + carry_part(q, 1))
-        return sums
+    def absorb(n, group, scaled, back, ritz):
+        for k in GROUPS[group]:
+            rows = rows_of(chip(k))
+            sums = []
+            for half in range(2):
+                total = []
+                for u in range(2):
+                    est = (estimate[half, u, rows] + scaled * resid[half, u, rows]) * back
+                    img = (image[half, u, rows] + scaled * turned[n + 1, half, u, rows]) * back
+                    estimate[half, u, rows] = est
+                    image[half, u, rows] = img
+                    res = img - ritz * est
+                    resid[half, u, rows] = res
+                    store_split(half, u, rows, res)
+                    total.append(jnp.sum((res * res).reshape(ROWS // 8, 8, TILE), axis=0))
+                sums.append(total[0] + total[1])
+            squares[chip(k)] = sums[0] + sums[1]
+        carry_rows(group)
 
     def take_in(n, phases, scaled, back, ritz):
-        phases[0][1]()
-        phases[0][2]()
-        first = absorb(n, 0, scaled, back, ritz)
-        phases[1][1]()
-        phases[1][2]()
-        second = absorb(n, 1, scaled, back, ritz)
-        return combine(first, second)
+        for forward, _, _ in phases:
+            forward()
+        for _, _, complete in phases:
+            complete(0)
+        absorb(n, 0, scaled, back, ritz)
+        for _, finish, _ in phases:
+            finish()
+        for _, _, complete in phases:
+            complete(1)
+        absorb(n, 1, scaled, back, ritz)
+        return jnp.sum(jnp.sum(squares[...], axis=0), axis=(0, 1), keepdims=True)
 
     for cp in inputs:
         cp.wait_send()
@@ -398,11 +447,20 @@
     for u in range(2):
         turned[0, 0, u, own_rows] = masked[:, u * TILE:(u + 1) * TILE]
         phases.append(gather_start(0, u))
+    pass_on(0, 0)
+    pass_on(0, 1)
     for forward, _, _ in phases:
         forward()
-    for _, finish, complete in phases:
+    for hop, i in ((0, 2), (1, 0)):
+        pass_on(hop, i)
+    left_cross[0].wait()
+    split_left(1)
+    pass_on(1, 1)
+    for _, finish, _ in phases:
         finish()
-        complete()
+    left_cross[1].wait()
+    split_left(3)
+    pass_on(1, 2)
 
     def first_split(half, u, rows):
         value = turned[0, half, u, rows]
@@ -413,17 +471,6 @@
         store_split(half, u, rows, value)
         return value * value
 
-    norm_square = combine(over_chunks(first_split, 0), over_chunks(first_split, 1))
-
-    for j in range(2):
-        local_left[j].wait()
-        left_cross[j].wait()
-    for q in range(4):
-        for k in range(RING):
-            hi, lo = split(lstage[q, rows_of(chip(k + 2))])
-            lhi[q, pl.ds(k * ROWS, ROWS)] = hi
-            llo[q, pl.ds(k * ROWS, ROWS)] = lo
-
     present = jnp.where(s + 1 < SECTIONS, 1.0, 0.0).astype(F32)
 
     def arrived(ref, sem):
@@ -459,7 +506,8 @@
             forwards.append(off_forward(j, piece))
             forwards[-1].start()
 
-    def first_carry(j, u):
+    def ready(j, u):
+        off_arrived(j, u)
         for q in (2 * j, 2 * j + 1):
             if q % 2:
                 for piece in ((0, 1) if u == 0 else (2,)):
@@ -469,34 +517,37 @@
                 arrived(corner.at[q], drecv.at[q])
                 put(q, 0, 0, 1, corner[q])
                 put(q, 1, 0, 0, corner[q].T)
-            carry(q, u)
-
-    off_arrived(0, 0)
+
+    ready(0, 0)
     put_diag(0)
-    first_carry(0, 0)
-    off_arrived(1, 0)
-    first_carry(1, 0)
+    for _, _, complete in phases:
+        complete(0)
+        complete(1)
+    norm_square = combine(over_chunks(first_split, 0), over_chunks(first_split, 1))
+    inverse = 1.0 / jnp.sqrt(norm_square)
+    carry(0, 0)
+    carry(1, 0)
+    ready(1, 0)
+    carry(2, 0)
+    carry(3, 0)
     products(0)
-    inverse = 1.0 / jnp.sqrt(norm_square)
     bend_share = bend_part(0, inverse)
-    off_arrived(0, 1)
     put_diag(1)
-    first_carry(0, 1)
+    for j in range(2):
+        ready(j, 1)
+        carry(2 * j, 1)
+        carry(2 * j + 1, 1)
     reduce_relay(0, 0)
-    off_arrived(1, 1)
-    first_carry(1, 1)
+    products(1)
+    send_bend(0, bend_share + bend_part(1, inverse))
     own_image(0, 0, resid[0, 0, own_rows])
     phases = [gather_start(1, 0)]
-    products(1)
-    send_bend(0, bend_share + bend_part(1, inverse))
-    phases[0][0]()
     reduce_relay(0, 1)
     own_image(0, 1, resid[0, 1, own_rows])
     phases.append(gather_start(1, 1))
     ritz = bend_total(0)
-    phases[1][0]()
     res_square = take_in(0, phases, inverse, 1.0, ritz)
-    for cp in shifts + forwards:
+    for cp in shifts + passed + forwards:
         cp.wait_send()
     for u in range(2):
         reduce_sent(0, u)
@@ -520,8 +571,6 @@
             own_image(n, u, resid[0, u, own_rows])
             phases.append(gather_start(n + 1, u))
         step, back, new_ritz = coefficients(ritz, res_square, bend_total(n))
-        for forward, _, _ in phases:
-            forward()
         new_square = take_in(n, phases, step * inverse, back, new_ritz)
         for u in range(2):
             reduce_sent(n, u)
@@ -573,7 +622,8 @@
             pltpu.VMEM((4, 2, HALF, HALF), BF16),
             pltpu.VMEM((4, PAD, HALF), BF16),
             pltpu.VMEM((4, PAD, HALF), BF16),
-            pltpu.VMEM((4, PAD, HALF), F32),
+            pltpu.VMEM((RING, 8, TILE), F32),
+            pltpu.VMEM((2, LONG_WAY, TILE, TILE), F32),
             pltpu.VMEM((ROWS, HALF), F32),
             pltpu.VMEM((ROWS, HALF), F32),
             pltpu.VMEM((ITERS + 1,) + full, F32),
@@ -586,10 +636,11 @@
             pltpu.VMEM((ITERS, 2, 7, ROWS, TILE), F32),
             pltpu.VMEM((ITERS + 1, 2 * RING, 1, TILE), F32),
             dma((2,)), dma((2, 2, 2)), dma((2,)), dma((2,)), dma((2,)), dma((2,)),
-            dma((2, 5)), dma((2, 2)), dma((2, 2)), dma((4,)), dma((4, 3)), dma((2, 3)),
+            dma((2, 4)), dma((2, 2)), dma((2, 2)), dma((4,)), dma((4, 3)), dma((2, 3)),
+            dma((3, LONG_WAY)), dma((2, LONG_WAY)),
             dma((ITERS, 2)), dma((ITERS, 2, 7)),
             dma((ITERS + 1, 2)), dma((ITERS + 1, 2, 7)),
-            dma((ITERS + 1, 2)), dma((ITERS + 1, 2)),
+            dma((ITERS + 1, 2)), dma((ITERS + 1, 2, 2)),
             dma((ITERS + 1,)), dma((ITERS + 1,)),
         ],
         compiler_params=pltpu.CompilerParams(

time: 146 us -> 140 us (0.959)
  Pallas kernels: 142 us -> 136 us
    pallas_call x1, Pallas kernels: 142 us -> 136 us  [per_device(): pl.pallas_call(kernel, out_shape=(jax.ShapeDtypeStruct((ROWS // 2, PAD),...]
where the time goes in v4:
time: 140 us
  Pallas kernels  136 us (97%)
  between operations  2.39 us (2%)
  local copies, waits for them, and re-layouts  1.47 us (1%)
    pallas_call x1, Pallas kernels, per_device(): pl.pallas_call(kernel, out_shape=(jax.ShapeDtypeStruct((ROWS // 2, PAD),...  136 us

profile of v4, /device:TPU:30, one launch (start us, length us, event | category | flops | bytes accessed | tf_op | source)
XLA Modules:
  0.0 139.5 jit_solution(6143866559978361920)
XLA Ops:
  0.6 135.7 %shard_map.68 = (f32[32,512]{1,0:T(8,128)}, f32[1]{0:T(128)}) custom-call(f32[32,512]{1,0:T(8,128)} %init_ref.1, f32[32,512]{1,0:T(8,128)} %site_ref.1, f32[1,2,512,512]{3,2,1,0:T(8,128)} %left_ref.1, f32[1,2,512,512]{3,2,1,0:T(8,128)} %right_ref.1, s32[1,2]{1,0:T(1,128)} %dims_ref.1), custom_call_target="tpu_custom_call" | custom-call | flops 16106127360 | bytes 8388608 | tf_op jit(solution)/shard_map/pallas_call | solution.py:604
  136.3 1.5 %copy.9 = f32[32,512]{1,0:T(8,128)} copy(f32[32,512]{1,0:T(8,128)} %get-tuple-element.4) | data formatting | bytes 131072

commit v5 on v4

--- a/solution.py
+++ b/solution.py
@@ -187,7 +187,7 @@
     shifts += [off_copy(0, 0), corner_copy(0, 0), corner_copy(0, 1)]
     shifts += [packed_copy(0, 0), packed_copy(1, 0)]
     shifts += [off_copy(1, 0), corner_copy(1, 0), corner_copy(1, 1)]
-    shifts += [packed_copy(0, 1), packed_copy(1, 1), off_copy(1, 2)]
+    shifts += [off_copy(1, 2), packed_copy(0, 1), packed_copy(1, 1)]
     for cp in shifts:
         cp.start()
     left_cross = [
@@ -281,13 +281,13 @@
         reduce_send(n, u, block(u, 7), 4, -1)
 
     def reduce_relay(n, u):
+        reduce_wait(n, u, 2)
+        block(u, 6)[...] = block(u, 6)[...] + rsbuf[n, u, 2]
+        reduce_send(n, u, block(u, 6), 6, -2)
         reduce_wait(n, u, 0)
         reduce_wait(n, u, 1)
         block(u, 2)[...] = block(u, 2)[...] + rsbuf[n, u, 0] + rsbuf[n, u, 1]
         reduce_send(n, u, block(u, 2), 5, 2)
-        reduce_wait(n, u, 2)
-        block(u, 6)[...] = block(u, 6)[...] + rsbuf[n, u, 2]
-        reduce_send(n, u, block(u, 6), 6, -2)
 
     def reduce_final(n, u):
         reduce_wait(n, u, 3)
@@ -347,12 +347,11 @@
         reduce_near(0, u)
 
     def operate(after_far):
-        for rows, then in ((far_rows, after_far), (near_rows, None)):
+        for rows, then in ((far_rows, after_far), (near_rows, lambda: None)):
             fresh = bring_back(rows, every)
             for u in range(2):
                 part[u, rows] = fresh[:, u * TILE:(u + 1) * TILE]
-            if then is not None:
-                then()
+            then()
 
     CHUNK = 128
 
@@ -532,11 +531,11 @@
     carry(3, 0)
     products(0)
     bend_share = bend_part(0, inverse)
-    put_diag(1)
     for j in range(2):
         ready(j, 1)
-        carry(2 * j, 1)
-        carry(2 * j + 1, 1)
+    put_diag(1)
+    for q in range(4):
+        carry(q, 1)
     reduce_relay(0, 0)
     products(1)
     send_bend(0, bend_share + bend_part(1, inverse))
@@ -578,7 +577,7 @@
 
     ritz, res_square = lax.fori_loop(1, ITERS, iterate, (ritz, res_square))
 
-    operate(None)
+    operate(lambda: None)
     inverse = 1.0 / jnp.sqrt(res_square)
     send_bend(ITERS, bend_part(0, inverse) + bend_part(1, inverse))
     step, back, ritz = coefficients(ritz, res_square, bend_total(ITERS))

time: 140 us -> 140 us (level)
  no operation moved by 1% of the time
where the time goes in v5:
time: 140 us; the launch traced here: 139 us
  Pallas kernels  136 us (97%)
  between operations  2.39 us (2%)
  local copies, waits for them, and re-layouts  1.47 us (1%)
    pallas_call x1, Pallas kernels, per_device(): pl.pallas_call(kernel, out_shape=(jax.ShapeDtypeStruct((ROWS // 2, PAD),...  136 us

profile of v5, /device:TPU:30, one launch (start us, length us, event | category | flops | bytes accessed | tf_op | source)
XLA Modules:
  0.0 139.5 jit_solution(7558440900577718893)
XLA Ops:
  0.6 135.6 %shard_map.68 = (f32[32,512]{1,0:T(8,128)}, f32[1]{0:T(128)}) custom-call(f32[32,512]{1,0:T(8,128)} %init_ref.1, f32[32,512]{1,0:T(8,128)} %site_ref.1, f32[1,2,512,512]{3,2,1,0:T(8,128)} %left_ref.1, f32[1,2,512,512]{3,2,1,0:T(8,128)} %right_ref.1, s32[1,2]{1,0:T(1,128)} %dims_ref.1), custom_call_target="tpu_custom_call" | custom-call | flops 16106127360 | bytes 8388608 | tf_op jit(solution)/shard_map/pallas_call | solution.py:603
  136.3 1.5 %copy.9 = f32[32,512]{1,0:T(8,128)} copy(f32[32,512]{1,0:T(8,128)} %get-tuple-element.4) | data formatting | bytes 131072

commit v6 on v5

--- a/solution.py
+++ b/solution.py
@@ -338,13 +338,6 @@
 
     far_rows, near_rows = slice(0, HALF), slice(HALF, PAD)
     every = slice(0, HALF)
-
-    def products(u):
-        cols = slice(u * TILE, (u + 1) * TILE)
-        part[u, far_rows] = bring_back(far_rows, cols)
-        reduce_far(0, u)
-        part[u, near_rows] = bring_back(near_rows, cols)
-        reduce_near(0, u)
 
     def operate(after_far):
         for rows, then in ((far_rows, after_far), (near_rows, lambda: None)):
@@ -529,21 +522,26 @@
     ready(1, 0)
     carry(2, 0)
     carry(3, 0)
-    products(0)
-    bend_share = bend_part(0, inverse)
     for j in range(2):
         ready(j, 1)
     put_diag(1)
     for q in range(4):
         carry(q, 1)
-    reduce_relay(0, 0)
-    products(1)
-    send_bend(0, bend_share + bend_part(1, inverse))
-    own_image(0, 0, resid[0, 0, own_rows])
-    phases = [gather_start(1, 0)]
-    reduce_relay(0, 1)
-    own_image(0, 1, resid[0, 1, own_rows])
-    phases.append(gather_start(1, 1))
+
+    def send_first():
+        for u in range(2):
+            reduce_far(0, u)
+
+    operate(send_first)
+    for u in range(2):
+        reduce_near(0, u)
+    send_bend(0, bend_part(0, inverse) + bend_part(1, inverse))
+    for u in range(2):
+        reduce_relay(0, u)
+    phases = []
+    for u in range(2):
+        own_image(0, u, resid[0, u, own_rows])
+        phases.append(gather_start(1, u))
     ritz = bend_total(0)
     res_square = take_in(0, phases, inverse, 1.0, ritz)
     for cp in shifts + passed + forwards:

time: 140 us -> 140 us (level)
  no operation moved by 1% of the time
where the time goes in v6:
time: 140 us
  Pallas kernels  136 us (97%)
  between operations  2.39 us (2%)
  local copies, waits for them, and re-layouts  1.47 us (1%)
    pallas_call x1, Pallas kernels, per_device(): pl.pallas_call(kernel, out_shape=(jax.ShapeDtypeStruct((ROWS // 2, PAD),...  136 us

profile of v6, /device:TPU:30, one launch (start us, length us, event | category | flops | bytes accessed | tf_op | source)
XLA Modules:
  0.0 140.1 jit_solution(76781218835208692)
XLA Ops:
  0.6 136.2 %shard_map.68 = (f32[32,512]{1,0:T(8,128)}, f32[1]{0:T(128)}) custom-call(f32[32,512]{1,0:T(8,128)} %init_ref.1, f32[32,512]{1,0:T(8,128)} %site_ref.1, f32[1,2,512,512]{3,2,1,0:T(8,128)} %left_ref.1, f32[1,2,512,512]{3,2,1,0:T(8,128)} %right_ref.1, s32[1,2]{1,0:T(1,128)} %dims_ref.1), custom_call_target="tpu_custom_call" | custom-call | flops 16106127360 | bytes 8388608 | tf_op jit(solution)/shard_map/pallas_call | solution.py:601
  136.8 1.5 %copy.9 = f32[32,512]{1,0:T(8,128)} copy(f32[32,512]{1,0:T(8,128)} %get-tuple-element.4) | data formatting | bytes 131072
